TPU v7x, 256 devices: a whole 4x4x8 slice. The times are simulated.
256 devices in a mesh: member: 4 (over y_lo, core), lat: 64 (over y_hi, z, x).
Axes of the slice: x: 4, y: 4 (y_hi: 2, y_lo: 2; y = y_hi * 2 + y_lo), z: 8, core: 2. Of those that a mesh axis runs over, the one named last changes fastest.
Arguments:
- latent: bfloat16 [8, 768, 128, 512], P('member', 'lat'), may hold values from -180 to 180
- noise: float32 [8, 32], P('member'), may hold values from -6 to 6
- noise_weight: float32 [32, 1024], replicated, may hold values from -0.5 to 0.5
- conv_weight: bfloat16 [9, 82, 512], replicated, may hold values from -0.09375 to 0.09375
- var_weight: float32 [82], replicated, may hold values from 0.2 to 5
- target: bfloat16 [82, 768, 128], P(None, 'lat'), may hold values from -6 to 6
- counts: int32 [64], replicated, may hold values from 1 to 12, 720 in all
Outputs:
- loss: float32 [], replicated
- band_loss: float32 [64], replicated
- grad_conv: float32 [9, 82, 512], replicated
- grad_noise: float32 [32, 1024], replicated
- grad_latent: bfloat16 [8, 768, 128, 512], P('member', 'lat')
Inputs may be any that keep to these rules, and one draw needn't show every extreme that they name: Band b's valid rows are its first counts[b] slots; the counts sum to 720 and one equals 12.
All inputs are finite; a program needn't handle non-finite values.
Results may differ from a plain program's by a relative error of at most 0.0045.
The roundings to bfloat16 on the way count: a program that leaves them out, or rounds other values in their place, can miss the bound.
Values may be sent and summed in bfloat16 or wider, within the bound.
A program may use at most 128 MiB of HBM per device.

v0:
```python
import jax
import jax.numpy as jnp
from jax import lax
from jax.sharding import PartitionSpec as P

EPSILON = 1e-05
SMOOTHING = 0.05


def from_behind(value, axis, steps):
    count = lax.axis_size(axis)
    initial, last = (max(0, -steps), min(count, count - steps))
    return lax.ppermute(value, axis, [(source, source + steps) for source in range(initial, last)])


def lookup(table, position):
    slots = jnp.arange(table.shape[0], dtype=jnp.int32)
    return jnp.sum(jnp.where(slots == position, table, 0))


def normalize(block):
    widened = block.astype(jnp.float32)
    average = jnp.mean(widened, -1, keepdims=True)
    centred = widened - average
    inv_std = lax.rsqrt(jnp.mean(centred * centred, -1, keepdims=True) + EPSILON)
    return (centred * inv_std, inv_std)


def pad_rows(own_rows, landing, leading, trailing, row_axis):
    first_pad = jnp.expand_dims(leading, row_axis)
    last_pad = jnp.expand_dims(trailing, row_axis)
    padded = jnp.concatenate([first_pad, own_rows, jnp.zeros_like(first_pad)], axis=row_axis)
    return jnp.where(landing, last_pad, padded)


def spread_taps(values_in):
    return jnp.concatenate(
        [jnp.roll(values_in, tap_col - 1, axis=-1) for tap_col in range(3)], axis=1
    )


def fold_taps(product, variables):
    result = jnp.roll(product[:, 0:variables], 1, axis=-1)
    result = result + product[:, variables : 2 * variables]
    return result + jnp.roll(product[:, 2 * variables : 3 * variables], -1, axis=-1)


def forward_conv(padded, tap_weights, band_rows, variables):
    decoded = 0.0
    for tap_row in range(3):
        product = jnp.einsum(
            "mrlc,kc->mkrl",
            padded[:, tap_row : tap_row + band_rows],
            tap_weights[tap_row],
            preferred_element_type=jnp.float32,
        )
        decoded = decoded + fold_taps(product, variables)
    return decoded


def crps_terms(mine, everyone, truth, weights, members_all):
    difference = mine - truth
    smooth_abs = jnp.sqrt(difference * difference + SMOOTHING * SMOOTHING)
    own_sum = smooth_abs - SMOOTHING
    own_slope = difference / smooth_abs
    pair_sum = jnp.zeros_like(mine)
    pair_slope = jnp.zeros_like(mine)
    for other in range(everyone.shape[0]):
        spread_diff = mine - everyone[other]
        pair_abs = jnp.sqrt(spread_diff * spread_diff + SMOOTHING * SMOOTHING)
        pair_sum = pair_sum + (pair_abs - SMOOTHING)
        pair_slope = pair_slope + spread_diff / pair_abs
    scores = own_sum / members_all - pair_sum / (2.0 * members_all * (members_all - 1))
    slopes = own_slope / members_all - pair_slope / (members_all * (members_all - 1))
    return ((weights * slopes).astype(jnp.bfloat16), jnp.sum(weights * scores))


def per_device(latent, noise, noise_weight, conv_weight, var_weight, target, counts):
    members_here, band_rows, lon_cells, channels = latent.shape
    variables = conv_weight.shape[1]
    members_all = float(members_here * lax.axis_size("member"))
    band_index = lax.axis_index("lat")
    live_count = lookup(counts, band_index)
    band_start = lookup(jnp.cumsum(counts) - counts, band_index)
    total_rows = jnp.sum(counts)
    rows_total = total_rows.astype(jnp.float32)
    row_ids = jnp.arange(band_rows, dtype=jnp.int32)
    live_rows = row_ids < live_count
    every_row = jnp.arange(counts.shape[0] * band_rows, dtype=jnp.int32)
    area_total = jnp.sum(
        jnp.where(
            every_row < total_rows,
            jnp.cos(jnp.pi * ((every_row.astype(jnp.float32) + 0.5) / rows_total - 0.5)),
            0.0,
        )
    )
    global_rows = (band_start + row_ids).astype(jnp.float32)
    area = jnp.where(live_rows, jnp.cos(jnp.pi * ((global_rows + 0.5) / rows_total - 0.5)), 0.0)
    row_scale = area * rows_total / (jnp.sum(var_weight) * area_total)
    band_weight = jnp.sum(row_scale) * jnp.sum(var_weight)
    weights = (var_weight[:, None] * row_scale[None, :])[:, :, None]
    modulation = jnp.dot(noise, noise_weight, precision=lax.Precision.HIGHEST)
    gain_part = modulation[:, None, None, :channels]
    shift_part = modulation[:, None, None, channels:]
    normed, inv_std = normalize(latent)
    live_mask = live_rows[None, :, None, None]
    mixed = jnp.where(live_mask, normed * (1.0 + gain_part) + shift_part, 0.0).astype(jnp.bfloat16)
    tap_weights = conv_weight.reshape(3, 3 * variables, channels)
    slot_ids = jnp.arange(band_rows + 2, dtype=jnp.int32)
    landing = slot_ids == live_count + 1
    last_row = lax.dynamic_index_in_dim(mixed, live_count - 1, axis=1, keepdims=False)
    first_row = mixed[:, 0]
    from_prev = from_behind(last_row, "lat", 1)
    from_next = from_behind(first_row, "lat", -1)
    padded = pad_rows(mixed, landing[None, :, None, None], from_prev, from_next, 1)
    decoded = forward_conv(padded, tap_weights, band_rows, variables)
    everyone = lax.all_gather(decoded, "member", axis=0, tiled=True)
    decoded_grad, loss_local = crps_terms(
        decoded, everyone, target.astype(jnp.float32), weights, members_all
    )
    band_slots = jnp.arange(counts.shape[0], dtype=jnp.int32)
    band_terms = jnp.where(band_slots == band_index, loss_local / (lon_cells * band_weight), 0.0)
    grad_last = lax.dynamic_index_in_dim(decoded_grad, live_count - 1, axis=2, keepdims=False)
    prev_grad = from_behind(grad_last, "lat", 1)
    next_grad = from_behind(decoded_grad[:, :, 0], "lat", -1)
    padded_grad = pad_rows(decoded_grad, landing[None, None, :, None], prev_grad, next_grad, 2)
    mixed_grad = 0.0
    for tap_row in range(3):
        window = spread_taps(padded_grad[:, :, 2 - tap_row : 2 - tap_row + band_rows])
        mixed_grad = mixed_grad + jnp.einsum(
            "mkrl,kc->mrlc", window, tap_weights[tap_row], preferred_element_type=jnp.float32
        )
    mixed_grad = jnp.where(live_mask, mixed_grad, 0.0)
    spread = spread_taps(decoded_grad)
    kernel_terms = jnp.stack(
        [
            jnp.einsum(
                "mkrl,mrlc->kc",
                spread,
                padded[:, tap_row : tap_row + band_rows],
                preferred_element_type=jnp.float32,
            )
            for tap_row in range(3)
        ]
    )
    gain_grad = jnp.sum(mixed_grad * normed, axis=(1, 2))
    shift_grad = jnp.sum(mixed_grad, axis=(1, 2))
    noise_terms = jnp.dot(
        noise.T, jnp.concatenate([gain_grad, shift_grad], axis=-1), precision=lax.Precision.HIGHEST
    )
    normed_grad = mixed_grad * (1.0 + gain_part)
    latent_grad = inv_std * (
        normed_grad
        - jnp.mean(normed_grad, -1, keepdims=True)
        - normed * jnp.mean(normed_grad * normed, -1, keepdims=True)
    )
    kernel_total, grad_noise, loss_total, band_loss = lax.psum(
        (kernel_terms, noise_terms, loss_local, band_terms), ("member", "lat")
    )
    loss = loss_total / (lon_cells * rows_total)
    grad_conv = kernel_total.reshape(9, variables, channels)
    return (loss, band_loss, grad_conv, grad_noise, latent_grad.astype(jnp.bfloat16))


def solution(mesh):
    return jax.shard_map(
        per_device,
        mesh=mesh,
        in_specs=(
            P("member", "lat", None, None),
            P("member", None),
            P(),
            P(),
            P(),
            P(None, "lat", None),
            P(),
        ),
        out_specs=(P(), P(), P(), P(), P("member", "lat", None, None)),
        check_vma=False,
    )
```

profile of v0, /device:TPU:1, one launch (start us, length us, event | category | flops | bytes accessed | tf_op | source)
XLA Modules:
  0.0 498.1 jit_solution(12807593905996373565)
XLA Ops:
  7.2 0.8 copy.14
  8.2 1.3 select_reduce_fusion.1
  11.5 2.5 convert_reduce_fusion
  14.3 1.3 fusion.14
  15.9 1.6 fusion.8
  17.6 1.7 copy-done.6
  19.2 0.8 slice_bitcast_fusion.8
  20.0 4.6 collective-permute-start.1
  24.7 1.3 collective-permute-start
  26.6 2.0 fusion.85
  28.6 1.7 reshape.134
  30.3 0.8 reshape.133
  31.1 1.0 reshape.132
  32.2 1.5 collective-permute-done
  33.7 2.4 maximum_select_fusion
  36.2 1.0 convolution_bitcast_fusion
  37.4 1.0 convolution_bitcast_fusion.1
  38.4 0.7 fusion.80
  39.1 1.7 fusion.79
  40.8 1.0 convolution_bitcast_fusion.2
  41.8 1.7 fusion.83
  43.5 1.7 fusion.84
  45.2 5.5 %fusion.60 = f32[2,82,12,128]{3,1,2,0:T(8,128)} fusion(f32[2,246,12,128]{3,1,2,0:T(8,128)S(1)} %convolution_bitcast_fusion, f32[2,246,12,128]{3,1,2,0:T(8,128)S(1)} %convolution_bitcast_fusion.1, f32[2,246,12,128]{3,1,2,0:T(8,128)S(1)} %convolution_bitcast_fusion.2, f32[2,82,12,127]{3,1,2,0:T(8,128)} %get-tuple-element.39, ...), kind=kLoop, calls=%fused_computation.66 | loop fusion | flops 3526656 | bytes 10076160 | tf_op jit(solution)/shard_map/add | solution.py:57
  51.7 1.8 convert_element_type.33
  54.1 1.3 select_reduce_fusion
  56.6 1.9 fusion.78
  60.0 47.1 %all-gather.2.cloned.1.call-done = f32[8,82,12,128]{3,1,2,0:T(8,128)} async-done(((f32[2,82,12,128]{3,1,2,0:T(8,128)}), f32[8,82,12,128]{3,1,2,0:T(8,128)}) %all-gather.2.cloned.1.call-update) | async-done | bytes 4030480 | tf_op jit(solution)/shard_map/all_gather | solution.py:117
  107.1 2.6 slice_bitcast_fusion.7
  109.7 5.7 %multiply_convert_fusion = (bf16[2,82,12,128]{3,1,2,0:T(8,128)(2,1)S(1)}, f32[]{:T(128)}) fusion(f32[2,82,12,128]{3,1,2,0:T(8,128)S(1)} %copy-done.7, f32[82,12,128]{2,0,1:T(8,128)S(1)} %get-tuple-element.21, f32[82,12,128]{2,0,1:T(8,128)S(1)} %get-tuple-element.22, f32[82,12,128]{2,0,1:T(8,128)S(1)} %get-tuple-element.23, ...), kind=kLoop, calls=%fused_computation.72 | loop fusion | flops 17381376 | bytes 6049636 | tf_op jit(solution)/shard_map/convert_element_type | solution.py:75
  115.4 0.7 slice_bitcast_fusion.9
  116.5 1.6 copy-done.3
  118.1 1.9 fusion.50
  120.0 1.9 fusion.53
  121.9 1.9 fusion.56
  123.8 3.1 collective-permute-start.3
  126.9 1.3 collective-permute-start.2
  128.8 2.6 pad_maximum_fusion
  131.4 80.2 %all-reduce = (f32[]{:T(128)}, f32[64]{0:T(128)}) all-reduce(f32[]{:T(128)} %get-tuple-element.19, f32[64]{0:T(128)S(1)} %fusion.73), channel_id=1, replica_groups=mesh['member'=4,'lat'=64] {'member','lat'}, use_global_device_ids=true, to_apply=%region_9.10 | all-reduce | flops 65 | bytes 520 | tf_op jit(solution)/shard_map/psum | solution.py:157
  211.7 2.5 reshape.131
  214.8 1.2 maximum_select_fusion.1
  217.6 0.7 copy-done.9
  218.3 2.2 fusion.31
  220.5 2.2 fusion.21
  222.7 7.3 %fusion.10 = (f32[2,12,128]{2,1,0:T(8,128)S(1)}, f32[2,512]{1,0:T(2,128)S(1)}, f32[2,12,128]{2,1,0:T(8,128)S(1)}, f32[2,512]{1,0:T(2,128)S(1)}, f32[2,12,128,512]{3,2,1,0:T(8,128)}) fusion(bf16[2,12,128,512]{3,2,1,0:T(8,128)(2,1)S(1)} %copy-done.4, f32[2,512]{1,0:T(2,128)S(1)} %get-tuple-element.66, f32[2,12,128]{2,1,0:T(8,128)S(1)} %copy-done.16, ...), kind=kOutput, calls=%fused_computation.12 | convolution fusion | flops 801845248 | bytes 23844876 | tf_op jit(solution)/shard_map/mkrl,kc->mrlc/dot_general | solution.py:130
  230.0 1.0 convolution_bitcast_fusion.3
  231.0 6.0 %fusion.13 = bf16[2,12,128,512]{3,2,1,0:T(8,128)(2,1)} fusion(bf16[2,12,128,512]{3,2,1,0:T(8,128)(2,1)S(1)} %copy-done.4, f32[2,12,128,512]{3,2,1,0:T(8,128)} %get-tuple-element.68, f32[2,12,128]{2,1,0:T(8,128)S(1)} %broadcast_multiply_fusion, f32[2,12,128]{2,1,0:T(8,128)S(1)} %broadcast_multiply_fusion.1, f32[2,512]{1,0:T(2,128)S(1)} %get-tuple-element.66, ...), kind=kLoop, calls=%fused_computation.15 | loop fusion | flops 14155776 | bytes 12636160 | tf_op jit(solution)/shard_map/convert_element_type | solution.py:162
  237.0 249.7 %all-reduce.4.cloned.1.call-done = (f32[9,82,512]{2,1,0:T(8,128)}, f32[32,1024]{1,0:T(8,128)}) async-done(((f32[9,82,512]{2,1,0:T(8,128)}, f32[32,1024]{1,0:T(8,128)}), (f32[9,82,512]{2,1,0:T(8,128)}, f32[32,1024]{1,0:T(8,128)})) %all-reduce.4.cloned.1.call-update) | async-done | bytes 1642512 | tf_op jit(solution)/shard_map/psum | solution.py:157
  486.7 2.7 copy.23
  (64 shorter events, 5.3 us)
Async XLA Ops:
  7.2 8.5 %copy-start = (f32[32,1024]{1,0:T(8,128)S(1)}, f32[32,1024]{1,0:T(8,128)}, u32[]{:S(2)}) copy-start(f32[32,1024]{1,0:T(8,128)} %param.9) | copy-start | bytes 393220
  7.2 99.9 %all-gather.2.cloned.1.call-start = ((), (), s32[]{:S(2)}) async-start(), calls=%async_computation | async-start | bytes 5406720 | tf_op jit(solution)/shard_map/all_gather | solution.py:117
  11.5 2.8 copy-start.4
  14.3 1.6 copy-start.13
  14.3 1.4 copy-start.18
  15.7 1.8 copy-start.15
  17.6 1.7 copy-start.6
  20.0 12.2 %collective-permute-start.1 = (bf16[2,128,512]{2,1,0:T(8,128)(2,1)}, bf16[2,128,512]{2,1,0:T(8,128)(2,1)}, u32[]{:S(2)}, u32[]{:S(2)}) collective-permute-start(bf16[2,128,512]{2,1,0:T(8,128)(2,1)} %get-tuple-element.29), channel_id=1, source_target_pairs={{0,1},{1,2},{2,3},{3,4},{4,5},{5,6},{6,7},{7,8},{8,9},{9,10},{10,1... | collective-permute-start | bytes 786440 | tf_op jit(solution)/shard_map/ppermute | solution.py:13
  24.7 9.1 %collective-permute-start = (bf16[2,128,512]{2,1,0:T(8,128)(2,1)}, bf16[2,128,512]{2,1,0:T(8,128)(2,1)}, u32[]{:S(2)}, u32[]{:S(2)}) collective-permute-start(bf16[2,128,512]{2,1,0:T(8,128)(2,1)} %get-tuple-element.28), channel_id=1, source_target_pairs={{1,0},{2,1},{3,2},{4,3},{5,4},{6,5},{7,6},{8,7},{9,8},{10,9},{11,1... | collective-permute-start | bytes 786440 | tf_op jit(solution)/shard_map/ppermute | solution.py:13
  33.7 2.4 copy-start.11
  36.1 4.7 copy-start.2
  36.1 1.2 copy-start.8
  50.8 2.7 copy-start.19
  50.8 435.9 %all-reduce.4.cloned.1.call-start = ((), (), s32[]{:S(2)}) async-start(), calls=%async_computation.1 | async-start | bytes 3506176 | tf_op jit(solution)/shard_map/psum | solution.py:157
  107.1 2.6 copy-start.7
  107.1 2.7 copy-start.10
  115.4 6.5 %copy-start.5 = (bf16[2,82,12,128]{3,1,2,0:T(8,128)(2,1)}, bf16[2,82,12,128]{3,1,2,0:T(8,128)(2,1)S(1)}, u32[]{:S(2)}) copy-start(bf16[2,82,12,128]{3,1,2,0:T(8,128)(2,1)S(1)} %get-tuple-element.18) | copy-start | bytes 1511428
  116.1 2.0 copy-start.3
  123.8 91.0 %collective-permute-start.3 = (bf16[2,82,128]{2,1,0:T(8,128)(2,1)}, bf16[2,82,128]{2,1,0:T(8,128)(2,1)S(1)}, u32[]{:S(2)}, u32[]{:S(2)}) collective-permute-start(bf16[2,82,128]{2,1,0:T(8,128)(2,1)} %get-tuple-element.61), channel_id=1, source_target_pairs={{0,1},{1,2},{2,3},{3,4},{4,5},{5,6},{6,7},{7,8},{8,9},{9,10},{10,1... | collective-permute-start | bytes 125960 | tf_op jit(solution)/shard_map/ppermute | solution.py:13
  126.9 87.9 %collective-permute-start.2 = (bf16[2,82,128]{2,1,0:T(8,128)(2,1)}, bf16[2,82,128]{2,1,0:T(8,128)(2,1)S(1)}, u32[]{:S(2)}, u32[]{:S(2)}) collective-permute-start(bf16[2,82,128]{2,1,0:T(8,128)(2,1)} %get-tuple-element.60), channel_id=1, source_target_pairs={{1,0},{2,1},{3,2},{4,3},{5,4},{6,5},{7,6},{8,7},{9,8},{10,9},{11,1... | collective-permute-start | bytes 125960 | tf_op jit(solution)/shard_map/ppermute | solution.py:13
  217.4 0.9 copy-start.9
  220.5 2.2 copy-start.12
  220.5 2.2 copy-start.14
  220.5 2.2 copy-start.16
  486.7 3.4 copy-start.1
  486.7 2.8 copy-start.17
Sparse Core Ops, SparseCore 0:
  50.9 56.1 all-gather.1
  231.2 255.4 all-reduce.3
where the time goes:
time: 500 us; the launch traced here: 498 us
  waiting for transfers between devices  298 us (60%)
  blocking collectives  80.2 us (16%)
  other arithmetic  36.7 us (7%)
  local copies, waits for them, and re-layouts  28.7 us (6%)
  between operations  22 us (4%)
  matrix products  21.5 us (4%)
  starting transfers between devices  10.6 us (2%)
    psum x1, waiting for transfers between devices, per_device(): lax.psum((kernel_terms, noise_terms, loss_local, band_terms), ('member',...  250 us
    psum x1, blocking collectives, per_device(): lax.psum((kernel_terms, noise_terms, loss_local, band_terms), ('member',...  80.2 us
    all_gather x1, waiting for transfers between devices, per_device(): everyone = lax.all_gather(decoded, 'member', axis=0, tiled=True)  47.1 us
    dot_general x3, matrix products, per_device(): jnp.einsum('mkrl,kc->mrlc', window, tap_weights[tap_row], preferred_eleme...  11.7 us
    ppermute x4, starting transfers between devices, from_behind(): lax.ppermute(value, axis, [(source, source + steps) for source in range(i...  10.3 us
  transfers between devices with their start and end apart: 6, of which 3 were waited for; matrix products, arithmetic and copies ran while one was open for 4% of the time, Pallas kernels for 0%

commit v1 on v0

v1 whole, which is shorter than its diff:
```python
import functools

import jax
import jax.numpy as jnp
from jax import lax
from jax.experimental import pallas as pl
from jax.experimental.pallas import tpu as pltpu
from jax.sharding import PartitionSpec as P

EPSILON = 1e-05
SMOOTHING = 0.05
C, V, LON, BAND = 512, 82, 128, 12
VP, KP = 88, 256
PAIR = 2 * VP
BANDS = 64
MESH = pl.DeviceIdType.MESH
NX, NY, NZ = 4, 4, 8
TILES = 32
SEMS = 128


class Place:
    def __init__(self):
        member, lat = lax.axis_index("member"), lax.axis_index("lat")
        self.member, self.lat = member, lat
        self.core = lax.rem(member, 2)
        self.x = lax.rem(lat, NX)
        self.z = lax.rem(lax.div(lat, NX), NZ)
        self.y = lax.div(lat, NX * NZ) * 2 + lax.div(member, 2)

    def at(self, **moved):
        x, y, z, core = (moved.get(n, getattr(self, n)) for n in ("x", "y", "z", "core"))
        return (lax.rem(y, 2) * 2 + core, (lax.div(y, 2) * NZ + z) * NX + x)

    def band(self, step):
        return (self.member, lax.rem(self.lat + step + BANDS, BANDS))

    def peers(self, axis):
        count = {"x": NX, "y": NY, "z": NZ, "core": 2}[axis]
        mine = getattr(self, axis)
        for k in range(1, count):
            there = lax.rem(mine + k, count)
            yield k, there, self.at(**{axis: there})


class Copies:
    def __init__(self, send_sem, recv_sem):
        self.send_sem, self.recv_sem, self.used, self.all = send_sem, recv_sem, 0, []

    def send(self, src, dst, device):
        i = self.used
        self.used += 1
        copy = pltpu.make_async_remote_copy(
            src_ref=src,
            dst_ref=dst,
            send_sem=self.send_sem.at[i],
            recv_sem=self.recv_sem.at[i],
            device_id=device,
            device_id_type=MESH,
        )
        copy.start()
        self.all.append(copy)
        return copy

    def finish(self):
        for copy in self.all:
            copy.wait_send()


def greet(place):
    devices = [d for axis in ("x", "y", "z", "core") for _, _, d in place.peers(axis)]
    devices += [place.at(y=there, core=1 - place.core) for _, there, _ in place.peers("y")]
    devices += [place.band(1), place.band(-1)]
    barrier = pltpu.get_barrier_semaphore()
    for device in devices:
        pl.semaphore_signal(barrier, inc=1, device_id=device, device_id_type=MESH)
    return lambda: pl.semaphore_wait(barrier, len(devices))


ORDERS = (("z", "x", "y"), ("x", "z", "y"), ("y", "z", "x"))
COUNT = {"x": NX, "y": NY, "z": NZ}


def nt_dot(a, b):
    return lax.dot_general(a, b, (((1,), (1,)), ((), ())), preferred_element_type=jnp.float32)


def nn_dot(a, b):
    return lax.dot_general(a, b, (((1,), (0,)), ((), ())), preferred_element_type=jnp.float32)


def rolled(value, steps):
    return pltpu.roll(value, steps % LON, 1)


def kernel(
    live, scale, latent, weight, noise_weight, noise, var_weight, target,
    conv_out, noise_out, band_out, latent_out,
    modulation, edges, edge_prod, edge_send, edge_in, normed, inv_std, mixed,
    product, decoded, decoded_half, part_in, cross_in, coef, grads, grads_out, score,
    grad_edge, grad_edge_in, stack, spread, turned, payload, mixed_grad, small,
    half, from_core, own, first, first_in, second, second_in, last, full, flat,
    small_z, small_x, small_y, noises, send_sem, recv_sem,
):
    f32, bf16 = jnp.float32, jnp.bfloat16
    place = Place()
    copies = Copies(send_sem, recv_sem)
    greeted = greet(place)
    count = live[0]
    final = jnp.maximum(count - 1, 0)
    core = place.core
    partner = place.at(core=1 - core)
    beside = place.y + 1 - 2 * lax.rem(place.y, 2)
    has_prev = place.lat > 0
    has_next = place.lat < BANDS - 1

    for i in range(2):
        for r in range(8):
            part = noise_weight[:, r * 128 : (r + 1) * 128] * noise[i]
            modulation[i, :, r * 128 : (r + 1) * 128] = jnp.sum(part, axis=0, keepdims=True)

    def normalize(block):
        widened = block.astype(f32)
        average = jnp.sum(widened, axis=-1, keepdims=True) * (1.0 / C)
        centred = widened - average
        rate = lax.rsqrt(jnp.sum(centred * centred, axis=-1, keepdims=True) * (1.0 / C) + EPSILON)
        return centred * rate, rate

    def modulate(value, i):
        return value * (1.0 + modulation[i, :, :C]) + modulation[i, :, C:]

    def fold(ref, lanes):
        value = rolled(ref[0:VP, lanes], 1)
        value = value + ref[V : V + VP, lanes]
        return value + rolled(ref[2 * V : 2 * V + VP, lanes], -1)

    for i in range(2):

        def edge_rows(n, carry, i=i):
            lon = pl.ds(pl.multiple_of(n * 32, 32), 32)
            for side, row in ((0, 0), (1, final)):
                value, _ = normalize(latent[i, row, lon, :])
                edges[side, i, lon, :] = modulate(value, i).astype(bf16)
            return carry

        lax.fori_loop(0, 4, edge_rows, 0)
    greeted()
    noises[place.member] = noise[...]
    noise_copies = [
        copies.send(noises.at[place.member], noises.at[place.member], device)
        for device in (partner, place.at(y=beside), place.at(y=beside, core=1 - core))
    ]
    edge_copies = []
    for side, a, step in ((0, 2, -1), (1, 0, 1)):
        edge_prod[...] = nt_dot(weight[a * KP : (a + 1) * KP, :], edges[side].reshape(2 * LON, C))
        for i in range(2):
            edge_send[side, i] = fold(edge_prod, slice(i * LON, (i + 1) * LON))
        edge_copies.append(copies.send(edge_send.at[side], edge_in.at[side], place.band(step)))

    for i in range(2):
        mixed[i, 0] = jnp.zeros((LON, C), bf16)
        mixed[i, BAND + 1] = jnp.zeros((LON, C), bf16)

        def rows(n, carry, i=i):
            row = lax.div(n, 4)
            lon = pl.ds(pl.multiple_of(lax.rem(n, 4) * 32, 32), 32)
            value, rate = normalize(latent[i, row, lon, :])
            normed[i, row, lon, :] = value
            inv_std[i, row, lon, :] = rate
            mixed[i, row + 1, lon, :] = jnp.where(row < count, modulate(value, i), 0.0).astype(bf16)
            return carry

        lax.fori_loop(0, BAND * 4, rows, 0, unroll=2)

    for copy in edge_copies:
        copy.wait_recv()
    part_copies, same_copies, other_copies = [], [], []
    for n in range(3):
        for mine in (False, True):
            pair = (core if mine else 1 - core) * 3 + n
            for i in range(2):
                value = None
                for a in range(3):
                    rows_in = mixed[i, pl.ds(2 * pair + a, 2)].reshape(2 * LON, C)
                    term = nt_dot(weight[a * KP : (a + 1) * KP, :], rows_in)
                    value = term if value is None else value + term
                product[i] = value
                for r in range(2):
                    row = 2 * pair + r
                    value = fold(product.at[i], slice(r * LON, (r + 1) * LON))
                    value = value + jnp.where((row == 0) & has_prev, edge_in[1, i], 0.0)
                    value = value + jnp.where((row == final) & has_next, edge_in[0, i], 0.0)
                    decoded[pair, i, r * VP : (r + 1) * VP, :] = value
                decoded_half[pair, i] = decoded[pair, i].astype(bf16)
            if mine:
                same_copies.append(
                    copies.send(decoded_half.at[pair], cross_in.at[n, core], place.at(y=beside))
                )
            else:
                other_copies.append(
                    copies.send(
                        decoded_half.at[pair], cross_in.at[n, core], place.at(y=beside, core=1 - core)
                    )
                )
                part_copies.append(copies.send(decoded.at[pair], part_in.at[n], partner))

    score[...] = jnp.zeros_like(score)
    grad_copies = []
    for n in range(3):
        pair = core * 3 + n
        for r in range(2):
            coef[r * VP : (r + 1) * VP, :] = var_weight[...] * scale[2 * pair + r]
        part_copies[n].wait_recv()
        same_copies[n].wait_recv()
        other_copies[n].wait_recv()

        def crps(k, carry, n=n, pair=pair):
            rows = pl.ds(pl.multiple_of(k * 16, 16), 16)
            mine = [decoded[pair, 0, rows, :], decoded[pair, 1, rows, :]]
            mine += [part_in[n, 0, rows, :], part_in[n, 1, rows, :]]
            truth = target[pair, rows, :].astype(f32)
            slopes, own_sum, pair_sum = [], 0.0, 0.0
            own_slopes = []
            for value in mine:
                d = value - truth
                square = d * d + SMOOTHING * SMOOTHING
                inverse = lax.rsqrt(square)
                own_slopes.append(d * inverse)
                own_sum = own_sum + (square * inverse - SMOOTHING)
                slopes.append(0.0)
            for j in range(4):
                for k2 in range(j + 1, 4):
                    d = mine[j] - mine[k2]
                    square = d * d + SMOOTHING * SMOOTHING
                    inverse = lax.rsqrt(square)
                    slope = d * inverse
                    slopes[j] = slopes[j] + slope
                    slopes[k2] = slopes[k2] - slope
                    pair_sum = pair_sum + 2.0 * (square * inverse - SMOOTHING)
            for c in range(2):
                for i in range(2):
                    theirs = cross_in[n, c, i, rows, :].astype(f32)
                    for j in range(4):
                        d = mine[j] - theirs
                        square = d * d + SMOOTHING * SMOOTHING
                        inverse = lax.rsqrt(square)
                        slopes[j] = slopes[j] + d * inverse
                        pair_sum = pair_sum + (square * inverse - SMOOTHING)
            weights = coef[rows, :]
            score[...] += weights * (own_sum * (1.0 / 8.0) - pair_sum * (1.0 / 112.0))
            for j in range(4):
                grad = weights * (own_slopes[j] * (1.0 / 8.0) - slopes[j] * (1.0 / 56.0))
                if j < 2:
                    grads[pair, j, rows, :] = grad.astype(bf16)
                else:
                    grads_out[n, j - 2, rows, :] = grad.astype(bf16)
            return carry

        lax.fori_loop(0, PAIR // 16, crps, 0)
        grad_copies.append(copies.send(grads_out.at[n], grads.at[pair], partner))

    for copy in grad_copies:
        copy.wait_recv()

    for i in range(2):
        edge_pair = grads[lax.div(final, 2), i].astype(f32)
        head = grads[0, i].astype(f32)[:VP]
        tail = jnp.where(lax.rem(final, 2) == 1, edge_pair[VP:], edge_pair[:VP])
        stack[0, i * VP : (i + 1) * VP, :] = head
        stack[1, i * VP : (i + 1) * VP, :] = tail
    grad_edge_copies = []
    for side, step in ((0, -1), (1, 1)):
        grad_edge[side] = stack[side, :PAIR].astype(bf16)
        grad_edge_copies.append(copies.send(grad_edge.at[side], grad_edge_in.at[side], place.band(step)))

    def spread_row(value, slot):
        stack[slot, 0:VP, :] = rolled(value, -1)
        stack[slot, V : V + VP, :] = value
        stack[slot, 2 * V : 2 * V + VP, :] = rolled(value, 1)
        stack[slot, 2 * V + VP :, :] = jnp.zeros((KP - 2 * V - VP, LON), f32)
        return stack[slot].astype(bf16)

    for i in range(2):
        spread[i, :, 0:LON] = jnp.zeros((KP, LON), bf16)
        spread[i, :, (BAND + 1) * LON :] = jnp.zeros((KP, LON), bf16)
        for pair in range(6):
            both = grads[pair, i].astype(f32)
            for r in range(2):
                slot = 2 * pair + r + 1
                value = spread_row(both[r * VP : (r + 1) * VP], slot % 4)
                spread[i, :, slot * LON : (slot + 1) * LON] = value
                turned[i, slot] = value.T

    for a in range(3):
        value = None
        for i in range(2):
            left = spread[i, :, (2 - a) * LON : (2 - a + BAND) * LON]
            term = nn_dot(left, mixed[i, 1 : BAND + 1].reshape(BAND * LON, C))
            value = term if value is None else value + term
        payload[a * KP : (a + 1) * KP, :] = value
    for copy in grad_edge_copies:
        copy.wait_recv()
    for side, a, there in ((1, 2, has_prev), (0, 0, has_next)):
        both = jnp.where(there, grad_edge_in[side].astype(f32), 0.0)
        values = [spread_row(both[i * VP : (i + 1) * VP], i) for i in range(2)]
        payload[a * KP : (a + 1) * KP, :] += nn_dot(
            jnp.concatenate(values, axis=1), edges[1 - side].reshape(2 * LON, C)
        )
        for i in range(2):
            flipped = values[i].T
            if side == 1:
                turned[i, 0] = flipped
            else:
                turned[i, BAND + 1] = jnp.zeros_like(flipped)
                for slot in range(2, BAND + 2):
                    turned[i, slot] = jnp.where(count + 1 == slot, flipped, turned[i, slot])

    small[...] = jnp.zeros_like(small)

    def backward(blocks):
        for block in blocks:
            i, pair = divmod(block, 6)
            value = None
            for a in range(3):
                left = turned[i, 2 * pair + 2 - a : 2 * pair + 4 - a].reshape(2 * LON, KP)
                term = nn_dot(left, weight[a * KP : (a + 1) * KP, :])
                value = term if value is None else value + term
            mixed_grad[...] = value.reshape(2, LON, C)

            def rows(n, carry, i=i, pair=pair):
                gain_sum, shift_sum = carry
                r = lax.div(n, 4)
                row = 2 * pair + r
                lon = pl.ds(pl.multiple_of(lax.rem(n, 4) * 32, 32), 32)
                grad = jnp.where(row < count, mixed_grad[r, lon, :], 0.0)
                value = normed[i, row, lon, :]
                times = grad * value
                gain_sum = gain_sum + jnp.sum(times.reshape(4, 8, C), axis=0)
                shift_sum = shift_sum + jnp.sum(grad.reshape(4, 8, C), axis=0)
                gain = 1.0 + modulation[i, :, :C]
                scaled = grad * gain
                mean = jnp.sum(scaled, axis=-1, keepdims=True) * (1.0 / C)
                along = jnp.sum(times * gain, axis=-1, keepdims=True) * (1.0 / C)
                result = inv_std[i, row, lon, :] * (scaled - mean - value * along)
                latent_out[i, row, lon, :] = result.astype(bf16)
                return gain_sum, shift_sum

            zero = jnp.zeros((8, C), f32)
            gain_sum, shift_sum = lax.fori_loop(0, 8, rows, (zero, zero), unroll=2)
            for k, total in ((0, gain_sum), (4, shift_sum)):
                line = jnp.sum(total, axis=0, keepdims=True)
                for q in range(4):
                    at = i * 8 + k + q
                    small[at : at + 1, :] += line[:, q * 128 : (q + 1) * 128]

    def tile(ref, row, piece):
        r, l = divmod(piece, 4)
        return ref[pl.ds(pl.multiple_of(row + r * 16, 16), 16), l * 128 : (l + 1) * 128]

    core_copies = []
    for s in range(3):
        for piece in range(TILES):
            half[s, piece] = tile(payload, (1 - core) * 384 + s * 128, piece)
        core_copies.append(copies.send(half.at[s], from_core.at[s], partner))
    backward(range(0, 2))

    stage1 = []
    for s, order in enumerate(ORDERS):
        g = TILES // COUNT[order[0]]
        core_copies[s].wait_recv()
        for piece in range(TILES):
            value = tile(payload, core * 384 + s * 128, piece) + from_core[s, piece]
            own[s, piece] = value
            first[s, piece] = value.astype(bf16)
        stage1.append([
            copies.send(first.at[s, pl.ds(j * g, g)], first_in.at[s, k - 1, pl.ds(0, g)], device)
            for k, j, device in place.peers(order[0])
        ])
    backward(range(2, 8))

    stage2 = []
    for s, order in enumerate(ORDERS):
        n = COUNT[order[0]]
        g = TILES // n
        me = getattr(place, order[0])
        for copy in stage1[s]:
            copy.wait_recv()
        for t in range(g):
            value = own[s, me * g + t]
            for k in range(n - 1):
                value = value + first_in[s, k, t].astype(f32)
            own[s, me * g + t] = value
            second[s, t] = value.astype(bf16)
        stage2.append([
            copies.send(second.at[s, pl.ds(j, 1)], second_in.at[s, pl.ds(k - 1, 1)], device)
            for k, j, device in place.peers(order[1])
        ])
    backward(range(8, 12))

    band = jnp.sum(jnp.sum(score[...], axis=1, keepdims=True), axis=0, keepdims=True)
    lanes = lax.broadcasted_iota(jnp.int32, (1, 128), 1)
    small[16:17, :] = jnp.where(lanes == place.lat, band, 0.0)
    small_copies = [
        copies.send(small, small_z.at[k - 1], device) for k, _, device in place.peers("z")
    ]

    stage3 = []
    for s, order in enumerate(ORDERS):
        n, n2 = COUNT[order[0]], COUNT[order[1]]
        g = TILES // n
        piece = getattr(place, order[0]) * g + getattr(place, order[1])
        for copy in stage2[s]:
            copy.wait_recv()
        value = own[s, piece]
        for k in range(n2 - 1):
            value = value + second_in[s, k].astype(f32)
        me = getattr(place, order[2])
        last[s, me] = value
        stage3.append([
            copies.send(last.at[s, me], last.at[s, me], device)
            for _, _, device in place.peers(order[2])
        ])

    for copy in small_copies:
        copy.wait_recv()
    total = small[...]
    for k in range(NZ - 1):
        total = total + small_z[k]
    small_x[place.x] = total
    small_copies = [
        copies.send(small_x.at[place.x], small_x.at[place.x], device)
        for _, _, device in place.peers("x")
    ]

    stage4 = []
    for s, order in enumerate(ORDERS):
        g = TILES // COUNT[order[0]]
        piece = getattr(place, order[0]) * g + getattr(place, order[1])
        for copy in stage3[s]:
            copy.wait_recv()
        value = last[s, 0] + last[s, 1] + last[s, 2] + last[s, 3]
        full[core, s, piece] = value.astype(bf16)
        stage4.append([
            copies.send(full.at[core, s, pl.ds(piece, 1)], full.at[core, s, pl.ds(piece, 1)], device)
            for _, _, device in place.peers(order[1])
        ])

    for copy in small_copies:
        copy.wait_recv()
    small_y[place.y, core] = small_x[0] + small_x[1] + small_x[2] + small_x[3]
    small_copies = [
        copies.send(small_y.at[place.y, core], small_y.at[place.y, core], device)
        for device in [partner]
        + [d for _, _, d in place.peers("y")]
        + [place.at(y=there, core=1 - core) for _, there, _ in place.peers("y")]
    ]

    stage5 = []
    for s, order in enumerate(ORDERS):
        g = TILES // COUNT[order[0]]
        me = getattr(place, order[0])
        for copy in stage4[s]:
            copy.wait_recv()
        stage5.append([
            copies.send(
                full.at[core, s, pl.ds(me * g, g)], full.at[core, s, pl.ds(me * g, g)], device
            )
            for _, _, device in place.peers(order[0])
        ])

    for copy in small_copies + noise_copies:
        copy.wait_recv()
    sums = [[small_y[y, c] + small_y[2 + y, c] for c in range(2)] for y in range(2)]
    band_out[...] = (sums[0][0][16:] + sums[0][1][16:]) + (sums[1][0][16:] + sums[1][1][16:])
    for r in range(8):
        value = jnp.zeros((32, 128), f32)
        for y in range(2):
            for c in range(2):
                for i in range(2):
                    line = sums[y][c][i * 8 + r : i * 8 + r + 1]
                    value = value + noises[y * 2 + c, i] * line
        noise_out[:, r * 128 : (r + 1) * 128] = value

    stage6 = []
    for s in range(3):
        for copy in stage5[s]:
            copy.wait_recv()
        stage6.append(copies.send(full.at[core, s], full.at[core, s], partner))
    for s in range(3):
        stage6[s].wait_recv()
        for c in range(2):
            for piece in range(TILES):
                r, l = divmod(piece, 4)
                row = c * 384 + s * 128 + r * 16
                flat[row : row + 16, l * 128 : (l + 1) * 128] = full[c, s, piece].astype(f32)
    for a in range(3):
        for b in range(3):
            conv_out[3 * a + b] = flat[a * KP + b * V : a * KP + b * V + V, :]
    copies.finish()


def run(live, scale, latent, weight, noise_weight, noise_wide, var_wide, truth):
    f32, bf16 = jnp.float32, jnp.bfloat16
    vmem = pl.BlockSpec(memory_space=pltpu.VMEM)
    smem = pl.BlockSpec(memory_space=pltpu.SMEM)
    scratch = [
        ((2, 1, 2 * C), f32),
        ((2, 2, LON, C), bf16),
        ((KP, 2 * LON), f32),
        ((2, 2, VP, LON), f32),
        ((2, 2, VP, LON), f32),
        ((2, BAND, LON, C), f32),
        ((2, BAND, LON, 1), f32),
        ((2, BAND + 2, LON, C), bf16),
        ((2, KP, 2 * LON), f32),
        ((6, 2, PAIR, LON), f32),
        ((6, 2, PAIR, LON), bf16),
        ((3, 2, PAIR, LON), f32),
        ((3, 2, 2, PAIR, LON), bf16),
        ((PAIR, LON), f32),
        ((6, 2, PAIR, LON), bf16),
        ((3, 2, PAIR, LON), bf16),
        ((16, LON), f32),
        ((2, PAIR, LON), bf16),
        ((2, PAIR, LON), bf16),
        ((4, KP, LON), f32),
        ((2, KP, (BAND + 2) * LON), bf16),
        ((2, BAND + 2, LON, KP), bf16),
        ((3 * KP, C), f32),
        ((2, LON, C), f32),
        ((24, 128), f32),
        ((3, TILES, 16, 128), f32),
        ((3, TILES, 16, 128), f32),
        ((3, TILES, 16, 128), f32),
        ((3, TILES, 16, 128), bf16),
        ((3, 7, 8, 16, 128), bf16),
        ((3, 8, 16, 128), bf16),
        ((3, 7, 16, 128), bf16),
        ((3, 4, 16, 128), f32),
        ((2, 3, TILES, 16, 128), bf16),
        ((3 * KP, C), f32),
        ((7, 24, 128), f32),
        ((4, 24, 128), f32),
        ((4, 2, 24, 128), f32),
        ((4, 2, 32, 128), f32),
    ]
    return pl.pallas_call(
        kernel,
        out_shape=(
            jax.ShapeDtypeStruct((9, V, C), f32),
            jax.ShapeDtypeStruct((32, 2 * C), f32),
            jax.ShapeDtypeStruct((8, 128), f32),
            jax.ShapeDtypeStruct((2, BAND, LON, C), bf16),
        ),
        in_specs=[smem] * 2 + [vmem] * 6,
        out_specs=(vmem,) * 4,
        scratch_shapes=[pltpu.VMEM(shape, dtype) for shape, dtype in scratch]
        + [pltpu.SemaphoreType.DMA((SEMS,))] * 2,
        compiler_params=pltpu.CompilerParams(
            collective_id=0, has_side_effects=True, vmem_limit_bytes=56 * 2**20
        ),
    )(live, scale, latent, weight, noise_weight, noise_wide, var_wide, truth)


def lookup(table, position):
    slots = jnp.arange(table.shape[0], dtype=jnp.int32)
    return jnp.sum(jnp.where(slots == position, table, 0))


def per_device(latent, noise, noise_weight, conv_weight, var_weight, target, counts):
    band_index = lax.axis_index("lat")
    rows_total = jnp.sum(counts).astype(jnp.float32)
    row_ids = jnp.arange(BAND, dtype=jnp.int32)
    starts = jnp.cumsum(counts) - counts
    slot_rows = (starts[:, None] + row_ids[None, :]).astype(jnp.float32)
    area = jnp.where(
        row_ids[None, :] < counts[:, None],
        jnp.cos(jnp.pi * ((slot_rows + 0.5) / rows_total - 0.5)),
        0.0,
    )
    band_scale = area * rows_total / (jnp.sum(var_weight) * jnp.sum(area))
    band_weight = jnp.sum(band_scale, axis=1) * jnp.sum(var_weight)
    here = jnp.arange(BANDS, dtype=jnp.int32) == band_index
    scale = jnp.sum(jnp.where(here[:, None], band_scale, 0.0), axis=0)
    live = lookup(counts, band_index).reshape(1)
    weight = jnp.pad(conv_weight.reshape(3, 3 * V, C), ((0, 0), (0, KP - 3 * V), (0, 0))).reshape(3 * KP, C)
    noise_wide = jnp.broadcast_to(noise[:, :, None], (2, 32, 128))
    var_wide = jnp.broadcast_to(jnp.pad(var_weight, (0, VP - V))[:, None], (VP, LON))
    truth = jnp.pad(target, ((0, VP - V), (0, 0), (0, 0))).transpose(1, 0, 2).reshape(6, PAIR, LON)
    grad_conv, grad_noise, band_sums, grad_latent = run(
        live, scale, latent, weight, noise_weight, noise_wide, var_wide, truth
    )
    band_sums = band_sums[0, :BANDS]
    loss = jnp.sum(band_sums) / (LON * rows_total)
    band_loss = band_sums / (LON * band_weight)
    return (loss, band_loss, grad_conv, grad_noise, grad_latent)


def solution(mesh):
    return jax.shard_map(
        per_device,
        mesh=mesh,
        in_specs=(
            P("member", "lat", None, None),
            P("member", None),
            P(),
            P(),
            P(),
            P(None, "lat", None),
            P(),
        ),
        out_specs=(P(), P(), P(), P(), P("member", "lat", None, None)),
        check_vma=False,
    )
```

time: 500 us -> 105 us (0.21)
  waiting for transfers between devices: 298 us -> 0 us
  blocking collectives: 80.2 us -> 0 us
  Pallas kernels: 0 us -> 78.5 us
  other arithmetic: 36.7 us -> 8.74 us
  matrix products: 21.5 us -> 0 us
  between operations: 22 us -> 4.4 us
  local copies, waits for them, and re-layouts: 28.7 us -> 13.3 us
  starting transfers between devices: 10.6 us -> 0 us
    psum x1 -> x0, waiting for transfers between devices: 250 us -> none  [per_device(): lax.psum((kernel_terms, noise_terms, loss_local, band_terms), ('member',...]
    psum x1 -> x0, blocking collectives: 80.2 us -> none  [per_device(): lax.psum((kernel_terms, noise_terms, loss_local, band_terms), ('member',...]
    pallas_call x0 -> x1, Pallas kernels: none -> 78.5 us  [run(): pl.pallas_call(kernel, out_shape=(jax.ShapeDtypeStruct((9, V, C), f32), j...]
    all_gather x1 -> x0, waiting for transfers between devices: 47.1 us -> none  [per_device(): everyone = lax.all_gather(decoded, 'member', axis=0, tiled=True)]
    dot_general x11 -> x0, matrix products: 21.5 us -> none  [the longest x3 11.7 us: per_device(): jnp.einsum('mkrl,kc->mrlc', window, tap_weights[tap_row], preferred_eleme...]
    convert_element_type x4 -> x0, other arithmetic: 15 us -> none  [the longest x1 5.98 us: per_device(): latent_grad.astype(jnp.bfloat16)]
    ppermute x4 -> x0, starting transfers between devices: 10.3 us -> none  [from_behind(): lax.ppermute(value, axis, [(source, source + steps) for source in range(i...]
    slice x10 -> x0, local copies, waits for them, and re-layouts: 9.72 us -> none  [the longest x4 5.81 us: fold_taps(): jnp.roll(product[:, 2 * variables:3 * variables], -1, axis=-1)]
  transfers between devices with their start and end apart: 6 -> 0, of which waited for: 3 -> 0; matrix products, arithmetic and copies ran while one was open for 4% -> 0% of each run, Pallas kernels for 0% -> 0%
where the time goes in v1:
time: 105 us
  Pallas kernels  78.5 us (75%)
  local copies, waits for them, and re-layouts  13.3 us (13%)
  other arithmetic  8.74 us (8%)
  between operations  4.4 us (4%)
    pallas_call x1, Pallas kernels, run(): pl.pallas_call(kernel, out_shape=(jax.ShapeDtypeStruct((9, V, C), f32), j...  78.5 us
    unnamed x5, local copies, waits for them, and re-layouts  5.94 us
    reduce_sum x2, other arithmetic, per_device(): band_scale = area * rows_total / (jnp.sum(var_weight) * jnp.sum(area))  2.61 us

profile of v1, /device:TPU:1, one launch (start us, length us, event | category | flops | bytes accessed | tf_op | source)
XLA Modules:
  0.0 104.9 jit_solution(5843199156703737378)
XLA Ops:
  0.6 1.3 %reduce_sum.69 = f32[]{:T(128)} reduce(f32[82]{0:T(128)} %param.11, f32[]{:T(128)} %constant.20.clone.1), dimensions={0}, to_apply=%region_3.4 | reduce | flops 81 | bytes 336 | tf_op jit(solution)/shard_map/reduce_sum | solution.py:581
  1.9 0.7 pad.13
  2.6 1.4 %broadcast_in_dim.38.noise = f32[2,32,128]{2,1,0:T(8,128)} broadcast(f32[2,32]{1,0:T(2,128)} %param.8), dimensions={0,1} | broadcast | bytes 33024 | tf_op jit(solution)/shard_map/broadcast_in_dim | solution.py:587
  3.9 0.7 copy.14
  4.7 0.1 reduce-window.9
  4.8 0.1 reduce.1
  4.9 1.3 %fusion.2 = (s32[]{:T(128)}, s32[]{:T(128)}, s32[64]{0:T(128)S(1)}) fusion(s32[64]{0:T(128)} %param.13, s32[]{:T(128)S(6)} %axis_index.12, s32[64]{0:T(128)S(1)} %reduce.1), kind=kLoop, calls=%fused_computation.10 | loop fusion | flops 318 | bytes 780 | tf_op jit(solution)/shard_map/reduce_sum | solution.py:572
  6.9 1.3 %fusion = f32[]{:T(128)} fusion(f32[]{:T(128)S(6)} %convert_element_type.13, s32[64]{0:T(128)S(1)} %get-tuple-element.17, s32[64]{0:T(128)} %param.13), kind=kLoop, calls=%fused_computation.4 | loop fusion | flops 6911 | bytes 520 | tf_op jit(solution)/shard_map/reduce_sum | solution.py:581
  9.5 1.3 %fusion.1 = (f32[64]{0:T(128)S(1)}, f32[12]{0:T(128)}) fusion(f32[]{:T(128)S(6)} %mul.31, f32[]{:T(128)S(6)} %convert_element_type.13, s32[64]{0:T(128)S(1)} %get-tuple-element.17, s32[64]{0:T(128)} %param.13, pred[64]{0:T(512)(128)(4,1)S(1)} %iota_compare_fusion.1), kind=kLoop, calls=%fused_computation.5 | loop fusion | flops 9908 | bytes 888 | tf_op jit(solution)/shard_map/reduce_sum | solution.py:582
  10.8 0.7 broadcast_in_dim.39.var_weight
  11.5 1.7 %pad.14 = bf16[88,12,128]{2,0,1:T(8,128)(2,1)} pad(bf16[82,12,128]{2,0,1:T(8,128)(2,1)} %param.12, bf16[]{:T(256)} %constant.21.clone.1), padding=0_6x0_0x0_0 | pad | bytes 522242 | tf_op jit(solution)/shard_map/jit(_pad)/pad | solution.py:589
  13.2 1.3 %reshape.59 = bf16[3,246,512]{2,1,0:T(8,128)(2,1)S(1)} reshape(bf16[9,82,512]{2,1,0:T(8,128)(2,1)} %param.10) | data formatting | bytes 1511424 | tf_op jit(solution)/shard_map/reshape | solution.py:586
  14.5 0.9 pad.12
  15.4 78.5 %shard_map.110 = (f32[9,82,512]{2,1,0:T(8,128)}, f32[32,1024]{1,0:T(8,128)}, f32[8,128]{1,0:T(8,128)}, bf16[2,12,128,512]{3,2,1,0:T(8,128)(2,1)}) custom-call(s32[1]{0:T(128)} %bitcast.live, f32[12]{0:T(128)} %get-tuple-element.14.scale, bf16[2,12,128,512]{3,2,1,0:T(8,128)(2,1)} %latent.1, bf16[768,512]{1,0:T(8,128)(2,1)} %bitcast.8, ...), custom_call_target="tpu_custom_call" | custom-call | tf_op jit(solution)/shard_map/pallas_call | solution.py:547
  93.9 0.0 copy-start
  93.9 1.4 %slice_reduce_fusion = f32[]{:T(128)} fusion(f32[8,128]{1,0:T(8,128)} %get-tuple-element.9), kind=kLoop, calls=%fused_computation.9 | loop fusion | flops 63 | bytes 260 | tf_op jit(solution)/shard_map/reduce_sum | solution.py:594
  96.0 1.8 %bitcast_divide_fusion = f32[64]{0:T(128)} fusion(f32[64]{0:T(128)S(1)} %get-tuple-element.13, f32[8,128]{1,0:T(8,128)} %get-tuple-element.9, f32[]{:T(128)} %reduce_sum.69), kind=kLoop, calls=%fused_computation.6 | loop fusion | flops 192 | bytes 772 | tf_op jit(solution)/shard_map/div | solution.py:595
  97.9 2.7 %copy.18 = f32[9,82,512]{2,1,0:T(8,128)} copy(f32[9,82,512]{2,1,0:T(8,128)} %get-tuple-element.25) | data formatting | bytes 3022848
  100.6 1.6 %copy.19 = f32[32,1024]{1,0:T(8,128)} copy(f32[32,1024]{1,0:T(8,128)} %get-tuple-element.26) | data formatting | bytes 262144
  102.1 0.0 copy-done
  102.1 1.7 %copy.20 = bf16[2,12,128,512]{3,2,1,0:T(8,128)(2,1)} copy(bf16[2,12,128,512]{3,2,1,0:T(8,128)(2,1)S(1)} %copy-done) | data formatting | bytes 6291456
  (1 shorter events, 0.0 us)
Async XLA Ops:
  93.9 8.2 %copy-start = (bf16[2,12,128,512]{3,2,1,0:T(8,128)(2,1)S(1)}, bf16[2,12,128,512]{3,2,1,0:T(8,128)(2,1)}, u32[]{:S(2)}) copy-start(bf16[2,12,128,512]{3,2,1,0:T(8,128)(2,1)} %get-tuple-element.27) | copy-start | bytes 9437188

commit v2 on v1

v2 whole, which is shorter than its diff:
```python
import functools

import jax
import jax.numpy as jnp
from jax import lax
from jax.experimental import pallas as pl
from jax.experimental.pallas import tpu as pltpu
from jax.sharding import PartitionSpec as P

EPSILON = 1e-05
SMOOTHING = 0.05
C, V, LON, BAND = 512, 82, 128, 12
VP, KP = 88, 256
PAIR = 2 * VP
BANDS = 64
MESH = pl.DeviceIdType.MESH
NX, NY, NZ = 4, 4, 8
TILES = 48
SEMS = 80


class Place:
    def __init__(self):
        member, lat = lax.axis_index("member"), lax.axis_index("lat")
        self.member, self.lat = member, lat
        self.core = lax.rem(member, 2)
        self.x = lax.rem(lat, NX)
        self.z = lax.rem(lax.div(lat, NX), NZ)
        self.y = lax.div(lat, NX * NZ) * 2 + lax.div(member, 2)

    def at(self, **moved):
        x, y, z, core = (moved.get(n, getattr(self, n)) for n in ("x", "y", "z", "core"))
        return (lax.rem(y, 2) * 2 + core, (lax.div(y, 2) * NZ + z) * NX + x)

    def band(self, step):
        return (self.member, lax.rem(self.lat + step + BANDS, BANDS))

    def peers(self, axis):
        count = {"x": NX, "y": NY, "z": NZ, "core": 2}[axis]
        mine = getattr(self, axis)
        for k in range(1, count):
            there = lax.rem(mine + k, count)
            yield k, there, self.at(**{axis: there})


class Copies:
    def __init__(self, send_sem, recv_sem):
        self.send_sem, self.recv_sem, self.used, self.all = send_sem, recv_sem, 0, []

    def send(self, src, dst, device):
        i = self.used
        self.used += 1
        copy = pltpu.make_async_remote_copy(
            src_ref=src,
            dst_ref=dst,
            send_sem=self.send_sem.at[i],
            recv_sem=self.recv_sem.at[i],
            device_id=device,
            device_id_type=MESH,
        )
        copy.start()
        self.all.append(copy)
        return copy

    def finish(self, but=0):
        ready = len(self.all) - but
        for copy in self.all[:ready]:
            copy.wait_send()
        self.all = self.all[ready:]


def greet(place):
    devices = [d for axis in ("x", "y", "z", "core") for _, _, d in place.peers(axis)]
    devices.append(place.at(y=place.y + 1 - 2 * lax.rem(place.y, 2), core=1 - place.core))
    devices += [place.band(1), place.band(-1)]
    barrier = pltpu.get_barrier_semaphore()
    for device in devices:
        pl.semaphore_signal(barrier, inc=1, device_id=device, device_id_type=MESH)
    return lambda: pl.semaphore_wait(barrier, len(devices))


SETS = (("x", "y"), ("y", "x"))
TAP_ROWS = (1, 2, 0)


def nt_dot(a, b):
    return lax.dot_general(a, b, (((1,), (1,)), ((), ())), preferred_element_type=jnp.float32)


def nn_dot(a, b):
    return lax.dot_general(a, b, (((1,), (0,)), ((), ())), preferred_element_type=jnp.float32)


def rolled(value, steps):
    return pltpu.roll(value, steps % LON, 1)


def kernel(
    counts, latent_hbm, conv_weight, noise_weight, noise_in, var_in, counts_in, target,
    full, noise_out, band_out, latent_hbm_out,
    latent, latent_out, weight, noise, var_weight, scale, norms, truth, modulation, edges, edge_prod, edge_send, edge_in, normed, inv_std, mixed,
    product, decoded, decoded_half, part_in, cross_in, coef, grads, grads_out, score,
    grad_edge, grad_edge_in, stack, spread, turned, pack, payload, mixed_grad, small,
    from_core, own, first, first_in, own2, second, second_in, over_z,
    small_x, small_y, small_c, noises, send_sem, recv_sem, local_sem,
):
    f32, bf16 = jnp.float32, jnp.bfloat16
    place = Place()
    copies = Copies(send_sem, recv_sem)
    greeted = greet(place)
    load = pltpu.make_async_copy(latent_hbm, latent, local_sem.at[0])
    load.start()
    count = counts[place.lat]
    final = jnp.maximum(count - 1, 0)
    core = place.core
    partner = place.at(core=1 - core)
    beside = place.y + 1 - 2 * lax.rem(place.y, 2)
    has_prev = place.lat > 0
    has_next = place.lat < BANDS - 1

    def column(row, size):
        across = lax.broadcasted_iota(jnp.int32, (size, size), 1)
        down = lax.broadcasted_iota(jnp.int32, (size, size), 0)
        return jnp.sum(jnp.where(across == down, row, 0), axis=1, keepdims=True)

    for a in range(3):
        for b in range(3):
            pack[b * V : (b + 1) * V, :] = conv_weight[3 * a + b].astype(f32)
        pack[3 * V :, :] = jnp.zeros((KP - 3 * V, C), f32)
        weight[a * KP : (a + 1) * KP, :] = pack[...].astype(bf16)

    var_total = jnp.sum(var_in[...], axis=1, keepdims=True)
    var_weight[...] = jnp.zeros_like(var_weight)
    var_weight[0:V, :] = jnp.broadcast_to(column(var_in[...], V), (V, LON))
    held = counts_in[...]
    before = lax.broadcasted_iota(jnp.int32, (BANDS, BANDS), 0) < lax.broadcasted_iota(
        jnp.int32, (BANDS, BANDS), 1
    )
    held_column = column(held.astype(f32), BANDS)
    starts = jnp.sum(jnp.where(before, held_column, 0.0), axis=0, keepdims=True)
    rows_total = jnp.sum(held.astype(f32), axis=1, keepdims=True)
    slots = lax.broadcasted_iota(jnp.int32, (16, BANDS), 0)
    angle = jnp.pi * ((starts + slots.astype(f32) + 0.5) / rows_total - 0.5)
    area = jnp.where(slots < held, jnp.cos(angle), 0.0)
    area_total = jnp.sum(jnp.sum(area, axis=1, keepdims=True), axis=0, keepdims=True)
    band_scale = area * rows_total / (var_total * area_total)
    norms[0:1, 0:BANDS] = LON * jnp.sum(band_scale, axis=0, keepdims=True) * var_total
    norms[1:2, :] = jnp.broadcast_to(LON * rows_total, (1, 128))
    here = lax.broadcasted_iota(jnp.int32, (16, BANDS), 1) == place.lat
    scale[...] = jnp.broadcast_to(
        jnp.sum(jnp.where(here, band_scale, 0.0), axis=1, keepdims=True), (16, LON)
    )
    truth[...] = jnp.zeros_like(truth)
    for i in range(2):
        noise[i] = jnp.broadcast_to(column(noise_in[i : i + 1, :], 32), (32, 128))

    for i in range(2):
        for r in range(8):
            part = noise_weight[:, r * 128 : (r + 1) * 128] * noise[i]
            modulation[i, :, r * 128 : (r + 1) * 128] = jnp.sum(part, axis=0, keepdims=True)

    def normalize(block):
        widened = block.astype(f32)
        average = jnp.sum(widened, axis=-1, keepdims=True) * (1.0 / C)
        centred = widened - average
        rate = lax.rsqrt(jnp.sum(centred * centred, axis=-1, keepdims=True) * (1.0 / C) + EPSILON)
        return centred * rate, rate

    def fold(ref, lanes):
        value = rolled(ref[0:VP, lanes], 1)
        value = value + ref[V : V + VP, lanes]
        return value + rolled(ref[2 * V : 2 * V + VP, lanes], -1)

    load.wait()

    def normalize_modulate(i, row, lon, gain, shift):
        value, rate = normalize(latent[i, row, lon, :])
        return value, rate, (value * gain + shift).astype(bf16)

    def edge_rows(n, carry):
        lon = pl.ds(pl.multiple_of(n * 32, 32), 32)
        for side, row in ((0, 0), (1, final)):
            for i in range(2):
                _, _, value = normalize_modulate(
                    i, row, lon, 1.0 + modulation[i, :, :C], modulation[i, :, C:]
                )
                edges[side, i, lon, :] = value
        return carry

    lax.fori_loop(0, 4, edge_rows, 0)
    greeted()
    noises[place.member] = noise[...]
    noise_copies = [
        copies.send(noises.at[place.member], noises.at[place.member], device)
        for device in (partner, place.at(y=beside), place.at(y=beside, core=1 - core))
    ]
    edge_copies = []
    for side, a, step in ((0, 2, -1), (1, 0, 1)):
        edge_prod[...] = nt_dot(weight[a * KP : (a + 1) * KP, :], edges[side].reshape(2 * LON, C))
        for i in range(2):
            edge_send[side, i] = fold(edge_prod, slice(i * LON, (i + 1) * LON))
        edge_copies.append(copies.send(edge_send.at[side], edge_in.at[side], place.band(step)))

    for i in range(2):
        mixed[i, 0] = jnp.zeros((LON, C), bf16)
        mixed[i, BAND + 1] = jnp.zeros((LON, C), bf16)

    def normalize_row(row, carry):
        for i in range(2):
            gain = jnp.where(row < count, 1.0 + modulation[i, :, :C], 0.0)
            shift = jnp.where(row < count, modulation[i, :, C:], 0.0)
            for part in range(4):
                lon = slice(part * 32, part * 32 + 32)
                value, rate, result = normalize_modulate(i, row, lon, gain, shift)
                normed[i, row, lon, :] = value
                inv_std[i, row, lon, :] = jnp.where(row < count, jnp.broadcast_to(rate, (32, LON)), 0.0)
                mixed[i, row + 1, lon, :] = result
        return carry

    part_copies, same_copies, other_copies = [], [], []
    for n in range(3):
        for begin, end in (((0, 3), (5, 9)), ((3, 5), (9, 11)), ((11, 12),))[n]:
            lax.fori_loop(begin, end, normalize_row, 0)
        for mine in (False, True):
            pair = (core if mine else 1 - core) * 3 + n
            for i in range(2):
                value = None
                for a in range(3):
                    rows_in = mixed[i, pl.ds(2 * pair + a, 2)].reshape(2 * LON, C)
                    term = nt_dot(weight[a * KP : (a + 1) * KP, :], rows_in)
                    value = term if value is None else value + term
                product[i] = value
            if n == 0 and not mine:
                for copy in edge_copies:
                    copy.wait_recv()
            for i in range(2):
                for r in range(2):
                    row = 2 * pair + r
                    value = fold(product.at[i], slice(r * LON, (r + 1) * LON))
                    value = value + jnp.where((row == 0) & has_prev, edge_in[1, i], 0.0)
                    value = value + jnp.where((row == final) & has_next, edge_in[0, i], 0.0)
                    decoded[pair, i, r * VP : (r + 1) * VP, :] = value
                decoded_half[pair, i] = decoded[pair, i].astype(bf16)
            if mine:
                same_copies.append(
                    copies.send(decoded_half.at[pair], cross_in.at[n, core], place.at(y=beside))
                )
            else:
                other_copies.append(
                    copies.send(
                        decoded_half.at[pair], cross_in.at[n, core], place.at(y=beside, core=1 - core)
                    )
                )
                part_copies.append(copies.send(decoded.at[pair], part_in.at[n], partner))

    def spread_row(value, slot):
        stack[slot, 0:VP, :] = rolled(value, -1)
        stack[slot, V : V + VP, :] = value
        stack[slot, 2 * V : 2 * V + VP, :] = rolled(value, 1)
        stack[slot, 2 * V + VP :, :] = jnp.zeros((KP - 2 * V - VP, LON), f32)
        return stack[slot].astype(bf16)

    def weigh(pair):
        for i in range(2):
            both = grads[pair, i].astype(f32)
            for r in range(2):
                value = spread_row(both[r * VP : (r + 1) * VP], 2 * i + r)
                spread[i, :, r * LON : (r + 1) * LON] = value
                turned[i, 2 * pair + r + 1] = value.T
        for a in range(3):
            value = payload[a * KP : (a + 1) * KP, :]
            for i in range(2):
                value = value + nn_dot(spread[i], mixed[i, pl.ds(2 * pair + a, 2)].reshape(2 * LON, C))
            payload[a * KP : (a + 1) * KP, :] = value

    score[...] = jnp.zeros_like(score)
    payload[...] = jnp.zeros_like(payload)
    grad_copies = []
    for n in range(3):
        pair = core * 3 + n
        for r in range(2):
            coef[r * VP : (r + 1) * VP, :] = var_weight[...] * scale[pl.ds(2 * pair + r, 1), :]
            truth[r * VP : r * VP + V, :] = target[2 * pair + r].astype(f32)
        part_copies[n].wait_recv()
        same_copies[n].wait_recv()
        other_copies[n].wait_recv()

        def crps(k, carry, n=n, pair=pair):
            rows = pl.ds(pl.multiple_of(k * 16, 16), 16)
            mine = [decoded[pair, 0, rows, :], decoded[pair, 1, rows, :]]
            mine += [part_in[n, 0, rows, :], part_in[n, 1, rows, :]]
            observed = truth[rows, :]
            slopes, own_sum, pair_sum = [], 0.0, 0.0
            own_slopes = []
            for value in mine:
                d = value - observed
                square = d * d + SMOOTHING * SMOOTHING
                inverse = lax.rsqrt(square)
                own_slopes.append(d * inverse)
                own_sum = own_sum + (square * inverse - SMOOTHING)
                slopes.append(0.0)
            for j in range(4):
                for k2 in range(j + 1, 4):
                    d = mine[j] - mine[k2]
                    square = d * d + SMOOTHING * SMOOTHING
                    inverse = lax.rsqrt(square)
                    slope = d * inverse
                    slopes[j] = slopes[j] + slope
                    slopes[k2] = slopes[k2] - slope
                    pair_sum = pair_sum + 2.0 * (square * inverse - SMOOTHING)
            for c in range(2):
                for i in range(2):
                    theirs = cross_in[n, c, i, rows, :].astype(f32)
                    for j in range(4):
                        d = mine[j] - theirs
                        square = d * d + SMOOTHING * SMOOTHING
                        inverse = lax.rsqrt(square)
                        slopes[j] = slopes[j] + d * inverse
                        pair_sum = pair_sum + (square * inverse - SMOOTHING)
            weights = coef[rows, :]
            score[...] += weights * (own_sum * (1.0 / 8.0) - pair_sum * (1.0 / 112.0))
            for j in range(4):
                grad = weights * (own_slopes[j] * (1.0 / 8.0) - slopes[j] * (1.0 / 56.0))
                if j < 2:
                    grads[pair, j, rows, :] = grad.astype(bf16)
                else:
                    grads_out[n, j - 2, rows, :] = grad.astype(bf16)
            return carry

        lax.fori_loop(0, PAIR // 16, crps, 0)
        grad_copies.append(copies.send(grads_out.at[n], grads.at[pair], partner))
        weigh(pair)
        if n > 0:
            grad_copies[n - 1].wait_recv()
            weigh((1 - core) * 3 + n - 1)
    grad_copies[2].wait_recv()

    for i in range(2):
        edge_pair = grads[lax.div(final, 2), i].astype(f32)
        head = grads[0, i].astype(f32)[:VP]
        tail = jnp.where(lax.rem(final, 2) == 1, edge_pair[VP:], edge_pair[:VP])
        stack[0, i * VP : (i + 1) * VP, :] = head
        stack[1, i * VP : (i + 1) * VP, :] = tail
    grad_edge_copies = []
    for side, step in ((0, -1), (1, 1)):
        grad_edge[side] = stack[side, :PAIR].astype(bf16)
        grad_edge_copies.append(copies.send(grad_edge.at[side], grad_edge_in.at[side], place.band(step)))

    weigh((1 - core) * 3 + 2)

    core_copies = [None] * 3

    def between_cores(s):
        rows = pl.ds(pl.multiple_of(s * KP + (1 - core) * 128, 128), 128)
        core_copies[s] = copies.send(payload.at[rows], from_core.at[s], partner)

    between_cores(1)
    for copy in grad_edge_copies:
        copy.wait_recv()
    for side, a, there in ((1, 2, has_prev), (0, 0, has_next)):
        both = jnp.where(there, grad_edge_in[side].astype(f32), 0.0)
        values = [spread_row(both[i * VP : (i + 1) * VP], 2 * side + i) for i in range(2)]
        payload[a * KP : (a + 1) * KP, :] += nn_dot(
            jnp.concatenate(values, axis=1), edges[1 - side].reshape(2 * LON, C)
        )
        between_cores(a)
        for i in range(2):
            flipped = values[i].T
            if side == 1:
                turned[i, 0] = flipped
            else:
                turned[i, BAND + 1] = jnp.zeros_like(flipped)
                for slot in range(2, BAND + 2):
                    turned[i, slot] = jnp.where(count + 1 == slot, flipped, turned[i, slot])

    small[...] = jnp.zeros_like(small)
    stores = []

    def points(i, r, row, part, gain_sum, shift_sum):
        lon = slice(part * 32, part * 32 + 32)
        grad = mixed_grad[r, lon, :]
        value = normed[i, row, lon, :]
        times = grad * value
        gain_sum = gain_sum + jnp.sum(times.reshape(4, 8, C), axis=0)
        shift_sum = shift_sum + jnp.sum(grad.reshape(4, 8, C), axis=0)
        gain = 1.0 + modulation[i, :, :C]
        scaled = grad * gain
        mean = jnp.sum(scaled, axis=-1, keepdims=True) * (1.0 / C)
        along = jnp.sum(times * gain, axis=-1, keepdims=True) * (1.0 / C)
        rate = inv_std[i, row, lon, :]
        result = jnp.concatenate([rate] * 4, axis=1) * (scaled - mean - value * along)
        latent_out[i, row, lon, :] = result.astype(bf16)
        return gain_sum, shift_sum

    def backward(blocks):
        for block in blocks:
            i, pair = divmod(block, 6)
            value = None
            for a in range(3):
                left = turned[i, 2 * pair + 2 - a : 2 * pair + 4 - a].reshape(2 * LON, KP)
                term = nn_dot(left, weight[a * KP : (a + 1) * KP, :])
                value = term if value is None else value + term
            mixed_grad[...] = value.reshape(2, LON, C)

            zero = jnp.zeros((8, C), f32)

            def rows(r, carry, i=i, pair=pair):
                gain_sum, shift_sum = carry
                row = 2 * pair + r
                gain_row, shift_row = zero, zero
                for part in range(4):
                    gain_row, shift_row = points(i, r, row, part, gain_row, shift_row)
                gain_sum = gain_sum + jnp.where(row < count, gain_row, 0.0)
                shift_sum = shift_sum + jnp.where(row < count, shift_row, 0.0)
                return gain_sum, shift_sum

            gain_sum, shift_sum = lax.fori_loop(0, 2, rows, (zero, zero))
            for k, total in ((0, gain_sum), (4, shift_sum)):
                line = jnp.sum(total, axis=0, keepdims=True)
                for q in range(4):
                    at = i * 8 + k + q
                    small[at : at + 1, :] += line[:, q * 128 : (q + 1) * 128]
            store = pltpu.make_async_copy(
                latent_out.at[i, 2 * pair : 2 * pair + 2],
                latent_hbm_out.at[i, 2 * pair : 2 * pair + 2],
                local_sem.at[1 + block],
            )
            store.start()
            stores.append(store)

    def tile(ref, row, lane):
        return ref[pl.ds(pl.multiple_of(row, 16), 16), lane * 128 : (lane + 1) * 128]

    def take_from_core(n):
        a = TAP_ROWS[n]
        core_copies[a].wait_recv()
        for r in range(8):
            group = n * 8 + r
            for lane in range(4):
                value = tile(payload, a * KP + core * 128 + r * 16, lane)
                value = value + tile(from_core.at[a], r * 16, lane)
                at = (group // 12, group % 12 * 4 + lane)
                own[at] = value
                first[at] = value.astype(bf16)

    def scatter(s, src, dst, size, axis):
        return [
            copies.send(src.at[s, pl.ds(j * size, size)], dst.at[s, k - 1], device)
            for k, j, device in place.peers(axis)
        ]

    take_from_core(0)
    take_from_core(1)
    stage1 = [scatter(0, first, first_in, 12, SETS[0][0])]
    take_from_core(2)
    stage1.append(scatter(1, first, first_in, 12, SETS[1][0]))
    backward(range(0, 6))

    stage2 = []
    for s in range(2):
        for copy in stage1[s]:
            copy.wait_recv()
        me = getattr(place, SETS[s][0])
        for t in range(12):
            value = own[s, me * 12 + t]
            for k in range(3):
                value = value + first_in[s, k, t].astype(f32)
            own2[s, t] = value
            second[s, t] = value.astype(bf16)
        stage2.append(scatter(s, second, second_in, 3, SETS[s][1]))
    backward(range(6, 12))

    for s in range(2):
        for copy in stage2[s]:
            copy.wait_recv()
        me = getattr(place, SETS[s][1])
        for t in range(3):
            value = own2[s, me * 3 + t]
            for k in range(3):
                value = value + second_in[s, k, t].astype(f32)
            over_z[place.z, s * 3 + t] = value.astype(bf16)
    band = jnp.sum(jnp.sum(score[...], axis=1, keepdims=True), axis=0, keepdims=True)
    lanes = lax.broadcasted_iota(jnp.int32, (1, 128), 1)
    small[16:17, :] = jnp.where(lanes == place.lat, band, 0.0)
    for t in range(2):
        value = small[t * 16 : (t + 1) * 16, :]
        coarse = value.astype(bf16)
        over_z[place.z, 6 + t] = coarse
        over_z[place.z, 8 + t] = (value - coarse.astype(f32)).astype(bf16)
    stage3 = [
        copies.send(over_z.at[place.z], over_z.at[place.z], device)
        for _, _, device in place.peers("z")
    ]
    for copy in stage3:
        copy.wait_recv()

    def piece(s):
        return getattr(place, SETS[s][0]) * 12 + getattr(place, SETS[s][1]) * 3

    def gather(s, start, size, axis):
        there = full.at[core, s, pl.ds(start, size)]
        return [copies.send(there, there, device) for _, _, device in place.peers(axis)]

    stage4 = []
    for s in range(2):
        for t in range(3):
            value = over_z[0, s * 3 + t].astype(f32)
            for z in range(1, NZ):
                value = value + over_z[z, s * 3 + t].astype(f32)
            full[core, s, piece(s) + t] = value.astype(bf16)
        stage4.append(gather(s, piece(s), 3, SETS[s][1]))
    for t in range(2):
        value = 0.0
        for z in range(NZ):
            value = value + (over_z[z, 6 + t].astype(f32) + over_z[z, 8 + t].astype(f32))
        small_x[place.x, t * 16 : (t + 1) * 16, :] = value
    small_copies = [
        copies.send(small_x.at[place.x], small_x.at[place.x], device)
        for _, _, device in place.peers("x")
    ]

    stage5 = []
    for s in range(2):
        for copy in stage4[s]:
            copy.wait_recv()
        stage5.append(gather(s, getattr(place, SETS[s][0]) * 12, 12, SETS[s][0]))
    for copy in small_copies:
        copy.wait_recv()
    small_y[place.y] = (small_x[0] + small_x[1]) + (small_x[2] + small_x[3])
    small_copies = [
        copies.send(small_y.at[place.y], small_y.at[place.y], device)
        for _, _, device in place.peers("y")
    ]
    copies.finish(but=9)

    for copy in small_copies:
        copy.wait_recv()
    small_c[core, 0] = small_y[0] + small_y[2]
    small_c[core, 1] = small_y[1] + small_y[3]
    small_copies = [copies.send(small_c.at[core], small_c.at[core], partner)]
    stage6 = []
    for s in range(2):
        for copy in stage5[s]:
            copy.wait_recv()
        stage6.append(copies.send(full.at[core, s], full.at[core, s], partner))
    for copy in small_copies + noise_copies:
        copy.wait_recv()
    sums = [[small_c[c, y] for c in range(2)] for y in range(2)]
    band_sums = (sums[0][0][16:17] + sums[0][1][16:17]) + (sums[1][0][16:17] + sums[1][1][16:17])
    band_out[...] = jnp.zeros_like(band_out)
    band_out[0:1, 0:BANDS] = band_sums[:, :BANDS] / norms[0:1, 0:BANDS]
    band_out[1:2, :] = jnp.sum(band_sums, axis=1, keepdims=True) / norms[1:2, :]
    for r in range(8):
        value = jnp.zeros((32, 128), f32)
        for y in range(2):
            for c in range(2):
                for i in range(2):
                    line = sums[y][c][i * 8 + r : i * 8 + r + 1]
                    value = value + noises[y * 2 + c, i] * line
        noise_out[:, r * 128 : (r + 1) * 128] = value

    for copy in stage6:
        copy.wait_recv()
    for store in stores:
        store.wait()
    copies.finish()


def write_kernel(full, noise_in, band_in, latent_in, conv_out, noise_out, band_out, loss_out, latent_out, flat, sem):
    moves = []
    for i in range(2):
        for part in range(4):
            rows = slice(part * 3, part * 3 + 3)
            moves.append(
                pltpu.make_async_copy(latent_in.at[i, rows], latent_out.at[i, rows], sem.at[i * 4 + part])
            )
            moves[-1].start()
    for s in range(2):
        for c in range(2):
            for t in range(TILES):
                n, r = divmod((s * 12 + t // 4) * 16, 128)
                row = TAP_ROWS[n] * KP + c * 128 + r
                lanes = slice(t % 4 * 128, t % 4 * 128 + 128)
                flat[row : row + 16, lanes] = full[c, s, t].astype(jnp.float32)
    for a in range(3):
        for b in range(3):
            conv_out[3 * a + b] = flat[a * KP + b * V : a * KP + b * V + V, :]
    noise_out[...] = noise_in[...]
    band_out[...] = band_in[0:1, 0:BANDS]
    loss_out[...] = band_in[1:2, 0:1]
    for move in moves:
        move.wait()


def per_device(latent, noise, noise_weight, conv_weight, var_weight, target, counts):
    f32, bf16 = jnp.float32, jnp.bfloat16
    vmem = pl.BlockSpec(memory_space=pltpu.VMEM)
    smem = pl.BlockSpec(memory_space=pltpu.SMEM)
    anywhere = pl.BlockSpec(memory_space=pl.ANY)
    scratch = [
        ((2, BAND, LON, C), bf16),
        ((2, BAND, LON, C), bf16),
        ((3 * KP, C), bf16),
        ((2, 32, 128), f32),
        ((VP, LON), f32),
        ((16, LON), f32),
        ((8, 128), f32),
        ((PAIR, LON), f32),
        ((2, 1, 2 * C), f32),
        ((2, 2, LON, C), bf16),
        ((KP, 2 * LON), f32),
        ((2, 2, VP, LON), f32),
        ((2, 2, VP, LON), f32),
        ((2, BAND, LON, C), f32),
        ((2, BAND, LON, LON), f32),
        ((2, BAND + 2, LON, C), bf16),
        ((2, KP, 2 * LON), f32),
        ((6, 2, PAIR, LON), f32),
        ((6, 2, PAIR, LON), bf16),
        ((3, 2, PAIR, LON), f32),
        ((3, 2, 2, PAIR, LON), bf16),
        ((PAIR, LON), f32),
        ((6, 2, PAIR, LON), bf16),
        ((3, 2, PAIR, LON), bf16),
        ((16, LON), f32),
        ((2, PAIR, LON), bf16),
        ((2, PAIR, LON), bf16),
        ((4, KP, LON), f32),
        ((2, KP, 2 * LON), bf16),
        ((2, BAND + 2, LON, KP), bf16),
        ((KP, C), f32),
        ((3 * KP, C), f32),
        ((2, LON, C), f32),
        ((32, 128), f32),
        ((3, 128, C), f32),
        ((2, TILES, 16, 128), f32),
        ((2, TILES, 16, 128), bf16),
        ((2, 3, 12, 16, 128), bf16),
        ((2, 12, 16, 128), f32),
        ((2, 12, 16, 128), bf16),
        ((2, 3, 3, 16, 128), bf16),
        ((NZ, 10, 16, 128), bf16),
        ((4, 32, 128), f32),
        ((4, 32, 128), f32),
        ((2, 2, 32, 128), f32),
        ((4, 2, 32, 128), f32),
    ]
    held = (
        jax.ShapeDtypeStruct((2, 2, TILES, 16, 128), bf16),
        jax.ShapeDtypeStruct((32, 2 * C), f32),
        jax.ShapeDtypeStruct((8, 128), f32),
        jax.ShapeDtypeStruct((2, BAND, LON, C), bf16),
    )
    results = pl.pallas_call(
        kernel,
        out_shape=held,
        in_specs=[smem, anywhere] + [vmem] * 6,
        out_specs=(vmem,) * 3 + (anywhere,),
        scratch_shapes=[pltpu.VMEM(shape, dtype) for shape, dtype in scratch]
        + [pltpu.SemaphoreType.DMA((SEMS,))] * 2
        + [pltpu.SemaphoreType.DMA((16,))],
        compiler_params=pltpu.CompilerParams(
            collective_id=0, has_side_effects=True, vmem_limit_bytes=56 * 2**20
        ),
    )(
        counts,
        latent,
        conv_weight,
        noise_weight,
        noise,
        var_weight.reshape(1, V),
        counts.reshape(1, BANDS),
        target.transpose(1, 0, 2),
    )
    grad_conv, grad_noise, band_loss, loss, grad_latent = pl.pallas_call(
        write_kernel,
        out_shape=(
            jax.ShapeDtypeStruct((9, V, C), f32),
            jax.ShapeDtypeStruct((32, 2 * C), f32),
            jax.ShapeDtypeStruct((1, BANDS), f32),
            jax.ShapeDtypeStruct((1, 1), f32),
            jax.ShapeDtypeStruct((2, BAND, LON, C), bf16),
        ),
        in_specs=[vmem] * 4,
        out_specs=(vmem,) * 4 + (anywhere,),
        scratch_shapes=[pltpu.VMEM((3 * KP, C), f32), pltpu.SemaphoreType.DMA((8,))],
        compiler_params=pltpu.CompilerParams(vmem_limit_bytes=60 * 2**20),
    )(*results)
    return (loss.reshape(()), band_loss.reshape(BANDS), grad_conv, grad_noise, grad_latent)


def solution(mesh):
    return jax.shard_map(
        per_device,
        mesh=mesh,
        in_specs=(
            P("member", "lat", None, None),
            P("member", None),
            P(),
            P(),
            P(),
            P(None, "lat", None),
            P(),
        ),
        out_specs=(P(), P(), P(), P(), P("member", "lat", None, None)),
        check_vma=False,
    )
```

time: 105 us -> 77.3 us (0.74)
  local copies, waits for them, and re-layouts: 13.3 us -> 0 us
  other arithmetic: 8.74 us -> 0 us
  between operations: 4.4 us -> 0.64 us
  Pallas kernels: 78.5 us -> 76.5 us
    reduce_sum x5 -> x0, other arithmetic: 6.7 us -> none  [the longest x2 2.61 us: per_device(): band_scale = area * rows_total / (jnp.sum(var_weight) * jnp.sum(area))]
    unnamed x5 -> x0, local copies, waits for them, and re-layouts: 5.94 us -> none
    pad x3 -> x0, local copies, waits for them, and re-layouts: 3.29 us -> none  [the longest x1 1.68 us: per_device(): jnp.pad(target, ((0, VP - V), (0, 0), (0, 0))).transpose(1, 0, 2)]
    broadcast_in_dim x2 -> x0, local copies, waits for them, and re-layouts: 2.06 us -> none  [the longest x1 1.36 us: per_device(): noise_wide = jnp.broadcast_to(noise[:, :, None], (2, 32, 128))]
    pallas_call x1 -> x2, Pallas kernels: 78.5 us -> 76.5 us  [the longest x1 71.4 us: per_device(): pl.pallas_call(kernel, out_shape=held, in_specs=[smem, anywhere] + [vmem]...]
    div x1 -> x0, other arithmetic: 1.83 us -> none  [per_device(): band_loss = band_sums / (LON * band_weight)]
    reshape x1 -> x0, local copies, waits for them, and re-layouts: 1.28 us -> none  [per_device(): conv_weight.reshape(3, 3 * V, C)]
where the time goes in v2:
time: 77.3 us; the launch traced here: 77.2 us
  Pallas kernels  76.5 us (99%)
    pallas_call x1, Pallas kernels, per_device(): pl.pallas_call(kernel, out_shape=held, in_specs=[smem, anywhere] + [vmem]...  71.4 us
    pallas_call x1, Pallas kernels, per_device(): pl.pallas_call(write_kernel, out_shape=(jax.ShapeDtypeStruct((9, V, C), f...  5.14 us

profile of v2, /device:TPU:1, one launch (start us, length us, event | category | flops | bytes accessed | tf_op | source)
XLA Modules:
  0.0 77.2 jit_solution(6784239750021434084)
XLA Ops:
  0.6 71.4 %shard_map.110 = (bf16[2,2,48,16,128]{4,3,2,1,0:T(8,128)(2,1)}, f32[32,1024]{1,0:T(8,128)}, f32[8,128]{1,0:T(8,128)}, bf16[2,12,128,512]{3,2,1,0:T(8,128)(2,1)}) custom-call(s32[64]{0:T(128)} %counts.1, bf16[2,12,128,512]{3,2,1,0:T(8,128)(2,1)} %latent_hbm.1, bf16[9,82,512]{2,1,0:T(8,128)(2,1)} %conv_weight.1, f32[32,1024]{1,0:T(8,128)} %noise_weight.1, ...), custom_call_target="tpu_custom_call" | custom-call | tf_op jit(solution)/shard_map/pallas_call | solution.py:654
  72.0 5.1 %shard_map.111 = (f32[9,82,512]{2,1,0:T(8,128)}, f32[32,1024]{1,0:T(8,128)}, f32[1,64]{1,0:T(1,128)}, f32[1,1]{1,0:T(1,128)}, bf16[2,12,128,512]{3,2,1,0:T(8,128)(2,1)}) custom-call(bf16[2,2,48,16,128]{4,3,2,1,0:T(8,128)(2,1)} %get-tuple-element.14.full, f32[32,1024]{1,0:T(8,128)} %get-tuple-element.15.noise_in, f32[8,128]{1,0:T(8,128)} %get-tuple-element.16.band_in, ...), custom_call_target="tpu_custom_call" | custom-call | tf_op jit(solution)/shard_map/pallas_call | solution.py:675

commit v3 on v2

--- a/solution.py
+++ b/solution.py
@@ -12,11 +12,11 @@
 C, V, LON, BAND = 512, 82, 128, 12
 VP, KP = 88, 256
 PAIR = 2 * VP
+VA = 96
 BANDS = 64
 MESH = pl.DeviceIdType.MESH
 NX, NY, NZ = 4, 4, 8
 TILES = 48
-SEMS = 80
 
 
 class Place:
@@ -69,10 +69,7 @@
         self.all = self.all[ready:]
 
 
-def greet(place):
-    devices = [d for axis in ("x", "y", "z", "core") for _, _, d in place.peers(axis)]
-    devices.append(place.at(y=place.y + 1 - 2 * lax.rem(place.y, 2), core=1 - place.core))
-    devices += [place.band(1), place.band(-1)]
+def greet(devices):
     barrier = pltpu.get_barrier_semaphore()
     for device in devices:
         pl.semaphore_signal(barrier, inc=1, device_id=device, device_id_type=MESH)
@@ -95,26 +92,34 @@
     return pltpu.roll(value, steps % LON, 1)
 
 
-def kernel(
+def spread_row(stack, value, slot):
+    stack[slot, 0:VP, :] = rolled(value, -1)
+    stack[slot, V : V + VP, :] = value
+    stack[slot, 2 * V : 2 * V + VP, :] = rolled(value, 1)
+    stack[slot, 2 * V + VP :, :] = jnp.zeros((KP - 2 * V - VP, LON), jnp.float32)
+    return stack[slot].astype(jnp.bfloat16)
+
+
+def front_kernel(
     counts, latent_hbm, conv_weight, noise_weight, noise_in, var_in, counts_in, target,
-    full, noise_out, band_out, latent_hbm_out,
-    latent, latent_out, weight, noise, var_weight, scale, norms, truth, modulation, edges, edge_prod, edge_send, edge_in, normed, inv_std, mixed,
-    product, decoded, decoded_half, part_in, cross_in, coef, grads, grads_out, score,
-    grad_edge, grad_edge_in, stack, spread, turned, pack, payload, mixed_grad, small,
-    from_core, own, first, first_in, own2, second, second_in, over_z,
-    small_x, small_y, small_c, noises, send_sem, recv_sem, local_sem,
+    payload, spread, normed, inv_std, modulation, edges, grads, score, norms, noises,
+    latent, forward_weight, noise, var_weight, scale, truth,
+    edge_prod, edge_send, edge_in, mixed,
+    product, decoded, decoded_half, part_in, cross_in, coef, grads_out,
+    stack, send_sem, recv_sem, local_sem,
 ):
     f32, bf16 = jnp.float32, jnp.bfloat16
     place = Place()
     copies = Copies(send_sem, recv_sem)
-    greeted = greet(place)
+    core = place.core
+    partner = place.at(core=1 - core)
+    beside = place.y + 1 - 2 * lax.rem(place.y, 2)
+    near = [partner, place.at(y=beside), place.at(y=beside, core=1 - core)]
+    greeted = greet(near + [place.band(1), place.band(-1)])
     load = pltpu.make_async_copy(latent_hbm, latent, local_sem.at[0])
     load.start()
     count = counts[place.lat]
     final = jnp.maximum(count - 1, 0)
-    core = place.core
-    partner = place.at(core=1 - core)
-    beside = place.y + 1 - 2 * lax.rem(place.y, 2)
     has_prev = place.lat > 0
     has_next = place.lat < BANDS - 1
 
@@ -123,11 +128,9 @@
         down = lax.broadcasted_iota(jnp.int32, (size, size), 0)
         return jnp.sum(jnp.where(across == down, row, 0), axis=1, keepdims=True)
 
-    for a in range(3):
-        for b in range(3):
-            pack[b * V : (b + 1) * V, :] = conv_weight[3 * a + b].astype(f32)
-        pack[3 * V :, :] = jnp.zeros((KP - 3 * V, C), f32)
-        weight[a * KP : (a + 1) * KP, :] = pack[...].astype(bf16)
+    for t in range(9):
+        forward_weight[t * VA + 80 : (t + 1) * VA, :] = jnp.zeros((VA - 80, C), bf16)
+        forward_weight[t * VA : t * VA + V, :] = conv_weight[t]
 
     var_total = jnp.sum(var_in[...], axis=1, keepdims=True)
     var_weight[...] = jnp.zeros_like(var_weight)
@@ -168,8 +171,8 @@
 
     def fold(ref, lanes):
         value = rolled(ref[0:VP, lanes], 1)
-        value = value + ref[V : V + VP, lanes]
-        return value + rolled(ref[2 * V : 2 * V + VP, lanes], -1)
+        value = value + ref[VA : VA + VP, lanes]
+        return value + rolled(ref[2 * VA : 2 * VA + VP, lanes], -1)
 
     load.wait()
 
@@ -192,11 +195,11 @@
     noises[place.member] = noise[...]
     noise_copies = [
         copies.send(noises.at[place.member], noises.at[place.member], device)
-        for device in (partner, place.at(y=beside), place.at(y=beside, core=1 - core))
+        for device in near
     ]
     edge_copies = []
     for side, a, step in ((0, 2, -1), (1, 0, 1)):
-        edge_prod[...] = nt_dot(weight[a * KP : (a + 1) * KP, :], edges[side].reshape(2 * LON, C))
+        edge_prod[...] = nt_dot(forward_weight[3 * a * VA : 3 * (a + 1) * VA, :], edges[side].reshape(2 * LON, C))
         for i in range(2):
             edge_send[side, i] = fold(edge_prod, slice(i * LON, (i + 1) * LON))
         edge_copies.append(copies.send(edge_send.at[side], edge_in.at[side], place.band(step)))
@@ -227,7 +230,7 @@
                 value = None
                 for a in range(3):
                     rows_in = mixed[i, pl.ds(2 * pair + a, 2)].reshape(2 * LON, C)
-                    term = nt_dot(weight[a * KP : (a + 1) * KP, :], rows_in)
+                    term = nt_dot(forward_weight[3 * a * VA : 3 * (a + 1) * VA, :], rows_in)
                     value = term if value is None else value + term
                 product[i] = value
             if n == 0 and not mine:
@@ -253,24 +256,16 @@
                 )
                 part_copies.append(copies.send(decoded.at[pair], part_in.at[n], partner))
 
-    def spread_row(value, slot):
-        stack[slot, 0:VP, :] = rolled(value, -1)
-        stack[slot, V : V + VP, :] = value
-        stack[slot, 2 * V : 2 * V + VP, :] = rolled(value, 1)
-        stack[slot, 2 * V + VP :, :] = jnp.zeros((KP - 2 * V - VP, LON), f32)
-        return stack[slot].astype(bf16)
-
     def weigh(pair):
         for i in range(2):
             both = grads[pair, i].astype(f32)
             for r in range(2):
-                value = spread_row(both[r * VP : (r + 1) * VP], 2 * i + r)
-                spread[i, :, r * LON : (r + 1) * LON] = value
-                turned[i, 2 * pair + r + 1] = value.T
+                value = spread_row(stack, both[r * VP : (r + 1) * VP], 2 * i + r)
+                spread[pair, i, :, r * LON : (r + 1) * LON] = value
         for a in range(3):
             value = payload[a * KP : (a + 1) * KP, :]
             for i in range(2):
-                value = value + nn_dot(spread[i], mixed[i, pl.ds(2 * pair + a, 2)].reshape(2 * LON, C))
+                value = value + nn_dot(spread[pair, i], mixed[i, pl.ds(2 * pair + a, 2)].reshape(2 * LON, C))
             payload[a * KP : (a + 1) * KP, :] = value
 
     score[...] = jnp.zeros_like(score)
@@ -335,6 +330,48 @@
             weigh((1 - core) * 3 + n - 1)
     grad_copies[2].wait_recv()
 
+    weigh((1 - core) * 3 + 2)
+    for copy in noise_copies:
+        copy.wait_recv()
+    copies.finish()
+
+
+def back_kernel(
+    counts, conv_weight, payload, spread, normed, inv_std, modulation, edges, grads, score, norms, noises,
+    full, noise_out, band_out, latent_out,
+    weight, grad_edge, grad_edge_in, stack, halo, turned, pack, fixed, mixed_grad, small,
+    from_core, own, first, first_in, own2, second, second_in, over_z,
+    small_z, small_x, small_y, small_c, send_sem, recv_sem,
+):
+    f32, bf16 = jnp.float32, jnp.bfloat16
+    place = Place()
+    copies = Copies(send_sem, recv_sem)
+    core = place.core
+    partner = place.at(core=1 - core)
+    greeted = greet(
+        [d for axis in ("x", "y", "z", "core") for _, _, d in place.peers(axis)]
+        + [place.band(1), place.band(-1)]
+    )
+    count = counts[place.lat]
+    final = jnp.maximum(count - 1, 0)
+    has_prev = place.lat > 0
+    has_next = place.lat < BANDS - 1
+
+    for a in range(3):
+        for b in range(3):
+            pack[b * V : (b + 1) * V, :] = conv_weight[3 * a + b].astype(f32)
+        pack[3 * V :, :] = jnp.zeros((KP - 3 * V, C), f32)
+        weight[a * KP : (a + 1) * KP, :] = pack[...].astype(bf16)
+
+    def turn_own():
+        for i in range(2):
+            for pair in range(6):
+                for r in range(2):
+                    turned[i, 2 * pair + r + 1] = spread[pair, i, :, r * LON : (r + 1) * LON].T
+
+    turn_own()
+    greeted()
+
     for i in range(2):
         edge_pair = grads[lax.div(final, 2), i].astype(f32)
         head = grads[0, i].astype(f32)[:VP]
@@ -346,35 +383,29 @@
         grad_edge[side] = stack[side, :PAIR].astype(bf16)
         grad_edge_copies.append(copies.send(grad_edge.at[side], grad_edge_in.at[side], place.band(step)))
 
-    weigh((1 - core) * 3 + 2)
-
     core_copies = [None] * 3
 
-    def between_cores(s):
-        rows = pl.ds(pl.multiple_of(s * KP + (1 - core) * 128, 128), 128)
-        core_copies[s] = copies.send(payload.at[rows], from_core.at[s], partner)
+    def tap_row(a):
+        return payload.at[KP : 2 * KP] if a == 1 else fixed.at[a // 2]
+
+    def between_cores(a):
+        rows = pl.ds(pl.multiple_of((1 - core) * 128, 128), 128)
+        core_copies[a] = copies.send(tap_row(a).at[rows], from_core.at[a], partner)
 
     between_cores(1)
     for copy in grad_edge_copies:
         copy.wait_recv()
     for side, a, there in ((1, 2, has_prev), (0, 0, has_next)):
         both = jnp.where(there, grad_edge_in[side].astype(f32), 0.0)
-        values = [spread_row(both[i * VP : (i + 1) * VP], 2 * side + i) for i in range(2)]
-        payload[a * KP : (a + 1) * KP, :] += nn_dot(
+        values = [spread_row(stack, both[i * VP : (i + 1) * VP], 2 * side + i) for i in range(2)]
+        fixed[a // 2] = payload[a * KP : (a + 1) * KP, :] + nn_dot(
             jnp.concatenate(values, axis=1), edges[1 - side].reshape(2 * LON, C)
         )
         between_cores(a)
         for i in range(2):
-            flipped = values[i].T
-            if side == 1:
-                turned[i, 0] = flipped
-            else:
-                turned[i, BAND + 1] = jnp.zeros_like(flipped)
-                for slot in range(2, BAND + 2):
-                    turned[i, slot] = jnp.where(count + 1 == slot, flipped, turned[i, slot])
+            halo[side, i] = values[i]
 
     small[...] = jnp.zeros_like(small)
-    stores = []
 
     def points(i, r, row, part, gain_sum, shift_sum):
         lon = slice(part * 32, part * 32 + 32)
@@ -392,6 +423,14 @@
         latent_out[i, row, lon, :] = result.astype(bf16)
         return gain_sum, shift_sum
 
+    def turn_halo():
+        for i in range(2):
+            turned[i, 0] = halo[1, i].T
+            trailing = halo[0, i].T
+            turned[i, BAND + 1] = jnp.where(count == BAND, trailing, jnp.zeros_like(trailing))
+            for slot in range(2, BAND + 1):
+                turned[i, slot] = jnp.where(count + 1 == slot, trailing, turned[i, slot])
+
     def backward(blocks):
         for block in blocks:
             i, pair = divmod(block, 6)
@@ -420,13 +459,6 @@
                 for q in range(4):
                     at = i * 8 + k + q
                     small[at : at + 1, :] += line[:, q * 128 : (q + 1) * 128]
-            store = pltpu.make_async_copy(
-                latent_out.at[i, 2 * pair : 2 * pair + 2],
-                latent_hbm_out.at[i, 2 * pair : 2 * pair + 2],
-                local_sem.at[1 + block],
-            )
-            store.start()
-            stores.append(store)
 
     def tile(ref, row, lane):
         return ref[pl.ds(pl.multiple_of(row, 16), 16), lane * 128 : (lane + 1) * 128]
@@ -437,7 +469,7 @@
         for r in range(8):
             group = n * 8 + r
             for lane in range(4):
-                value = tile(payload, a * KP + core * 128 + r * 16, lane)
+                value = tile(tap_row(a), core * 128 + r * 16, lane)
                 value = value + tile(from_core.at[a], r * 16, lane)
                 at = (group // 12, group % 12 * 4 + lane)
                 own[at] = value
@@ -454,7 +486,8 @@
     stage1 = [scatter(0, first, first_in, 12, SETS[0][0])]
     take_from_core(2)
     stage1.append(scatter(1, first, first_in, 12, SETS[1][0]))
-    backward(range(0, 6))
+    turn_halo()
+    backward(range(0, 4))
 
     stage2 = []
     for s in range(2):
@@ -468,7 +501,7 @@
             own2[s, t] = value
             second[s, t] = value.astype(bf16)
         stage2.append(scatter(s, second, second_in, 3, SETS[s][1]))
-    backward(range(6, 12))
+    backward(range(4, 7))
 
     for s in range(2):
         for copy in stage2[s]:
@@ -479,18 +512,11 @@
             for k in range(3):
                 value = value + second_in[s, k, t].astype(f32)
             over_z[place.z, s * 3 + t] = value.astype(bf16)
-    band = jnp.sum(jnp.sum(score[...], axis=1, keepdims=True), axis=0, keepdims=True)
-    lanes = lax.broadcasted_iota(jnp.int32, (1, 128), 1)
-    small[16:17, :] = jnp.where(lanes == place.lat, band, 0.0)
-    for t in range(2):
-        value = small[t * 16 : (t + 1) * 16, :]
-        coarse = value.astype(bf16)
-        over_z[place.z, 6 + t] = coarse
-        over_z[place.z, 8 + t] = (value - coarse.astype(f32)).astype(bf16)
     stage3 = [
         copies.send(over_z.at[place.z], over_z.at[place.z], device)
         for _, _, device in place.peers("z")
     ]
+    backward(range(7, 10))
     for copy in stage3:
         copy.wait_recv()
 
@@ -509,14 +535,15 @@
                 value = value + over_z[z, s * 3 + t].astype(f32)
             full[core, s, piece(s) + t] = value.astype(bf16)
         stage4.append(gather(s, piece(s), 3, SETS[s][1]))
-    for t in range(2):
-        value = 0.0
-        for z in range(NZ):
-            value = value + (over_z[z, 6 + t].astype(f32) + over_z[z, 8 + t].astype(f32))
-        small_x[place.x, t * 16 : (t + 1) * 16, :] = value
+    backward(range(10, 12))
+
+    band = jnp.sum(jnp.sum(score[...], axis=1, keepdims=True), axis=0, keepdims=True)
+    lanes = lax.broadcasted_iota(jnp.int32, (1, 128), 1)
+    small[16:17, :] = jnp.where(lanes == place.lat, band, 0.0)
+    small_z[place.z] = small[...]
     small_copies = [
-        copies.send(small_x.at[place.x], small_x.at[place.x], device)
-        for _, _, device in place.peers("x")
+        copies.send(small_z.at[place.z], small_z.at[place.z], device)
+        for _, _, device in place.peers("z")
     ]
 
     stage5 = []
@@ -526,12 +553,22 @@
         stage5.append(gather(s, getattr(place, SETS[s][0]) * 12, 12, SETS[s][0]))
     for copy in small_copies:
         copy.wait_recv()
+    total = small_z[0]
+    for z in range(1, NZ):
+        total = total + small_z[z]
+    small_x[place.x] = total
+    small_copies = [
+        copies.send(small_x.at[place.x], small_x.at[place.x], device)
+        for _, _, device in place.peers("x")
+    ]
+    for copy in small_copies:
+        copy.wait_recv()
     small_y[place.y] = (small_x[0] + small_x[1]) + (small_x[2] + small_x[3])
     small_copies = [
         copies.send(small_y.at[place.y], small_y.at[place.y], device)
         for _, _, device in place.peers("y")
     ]
-    copies.finish(but=9)
+    copies.finish(but=12)
 
     for copy in small_copies:
         copy.wait_recv()
@@ -543,7 +580,7 @@
         for copy in stage5[s]:
             copy.wait_recv()
         stage6.append(copies.send(full.at[core, s], full.at[core, s], partner))
-    for copy in small_copies + noise_copies:
+    for copy in small_copies:
         copy.wait_recv()
     sums = [[small_c[c, y] for c in range(2)] for y in range(2)]
     band_sums = (sums[0][0][16:17] + sums[0][1][16:17]) + (sums[1][0][16:17] + sums[1][1][16:17])
@@ -561,8 +598,6 @@
 
     for copy in stage6:
         copy.wait_recv()
-    for store in stores:
-        store.wait()
     copies.finish()
 
 
@@ -597,41 +632,49 @@
     vmem = pl.BlockSpec(memory_space=pltpu.VMEM)
     smem = pl.BlockSpec(memory_space=pltpu.SMEM)
     anywhere = pl.BlockSpec(memory_space=pl.ANY)
-    scratch = [
+    between = [
+        ((3 * KP, C), f32),
+        ((6, 2, KP, 2 * LON), bf16),
+        ((2, BAND, LON, C), f32),
+        ((2, BAND, LON, LON), f32),
+        ((2, 1, 2 * C), f32),
+        ((2, 2, LON, C), bf16),
+        ((6, 2, PAIR, LON), bf16),
+        ((16, LON), f32),
+        ((8, 128), f32),
+        ((4, 2, 32, 128), f32),
+    ]
+    front_scratch = [
         ((2, BAND, LON, C), bf16),
-        ((2, BAND, LON, C), bf16),
-        ((3 * KP, C), bf16),
+        ((9 * VA, C), bf16),
         ((2, 32, 128), f32),
         ((VP, LON), f32),
         ((16, LON), f32),
-        ((8, 128), f32),
         ((PAIR, LON), f32),
-        ((2, 1, 2 * C), f32),
-        ((2, 2, LON, C), bf16),
-        ((KP, 2 * LON), f32),
+        ((3 * VA, 2 * LON), f32),
         ((2, 2, VP, LON), f32),
         ((2, 2, VP, LON), f32),
-        ((2, BAND, LON, C), f32),
-        ((2, BAND, LON, LON), f32),
         ((2, BAND + 2, LON, C), bf16),
-        ((2, KP, 2 * LON), f32),
+        ((2, 3 * VA, 2 * LON), f32),
         ((6, 2, PAIR, LON), f32),
         ((6, 2, PAIR, LON), bf16),
         ((3, 2, PAIR, LON), f32),
         ((3, 2, 2, PAIR, LON), bf16),
         ((PAIR, LON), f32),
-        ((6, 2, PAIR, LON), bf16),
         ((3, 2, PAIR, LON), bf16),
-        ((16, LON), f32),
+        ((4, KP, LON), f32),
+    ]
+    back_scratch = [
+        ((3 * KP, C), bf16),
         ((2, PAIR, LON), bf16),
         ((2, PAIR, LON), bf16),
         ((4, KP, LON), f32),
-        ((2, KP, 2 * LON), bf16),
+        ((2, 2, KP, LON), bf16),
         ((2, BAND + 2, LON, KP), bf16),
         ((KP, C), f32),
-        ((3 * KP, C), f32),
+        ((2, KP, C), f32),
         ((2, LON, C), f32),
-        ((32, 128), f32),
+        ((24, 128), f32),
         ((3, 128, C), f32),
         ((2, TILES, 16, 128), f32),
         ((2, TILES, 16, 128), bf16),
@@ -639,28 +682,22 @@
         ((2, 12, 16, 128), f32),
         ((2, 12, 16, 128), bf16),
         ((2, 3, 3, 16, 128), bf16),
-        ((NZ, 10, 16, 128), bf16),
-        ((4, 32, 128), f32),
-        ((4, 32, 128), f32),
-        ((2, 2, 32, 128), f32),
-        ((4, 2, 32, 128), f32),
+        ((NZ, 6, 16, 128), bf16),
+        ((NZ, 24, 128), f32),
+        ((4, 24, 128), f32),
+        ((4, 24, 128), f32),
+        ((2, 2, 24, 128), f32),
     ]
-    held = (
-        jax.ShapeDtypeStruct((2, 2, TILES, 16, 128), bf16),
-        jax.ShapeDtypeStruct((32, 2 * C), f32),
-        jax.ShapeDtypeStruct((8, 128), f32),
-        jax.ShapeDtypeStruct((2, BAND, LON, C), bf16),
-    )
-    results = pl.pallas_call(
-        kernel,
-        out_shape=held,
+    handed = pl.pallas_call(
+        front_kernel,
+        out_shape=[pltpu.VMEM(shape, dtype) for shape, dtype in between],
         in_specs=[smem, anywhere] + [vmem] * 6,
-        out_specs=(vmem,) * 3 + (anywhere,),
-        scratch_shapes=[pltpu.VMEM(shape, dtype) for shape, dtype in scratch]
-        + [pltpu.SemaphoreType.DMA((SEMS,))] * 2
-        + [pltpu.SemaphoreType.DMA((16,))],
+        out_specs=[vmem] * len(between),
+        scratch_shapes=[pltpu.VMEM(shape, dtype) for shape, dtype in front_scratch]
+        + [pltpu.SemaphoreType.DMA((24,))] * 2
+        + [pltpu.SemaphoreType.DMA((1,))],
         compiler_params=pltpu.CompilerParams(
-            collective_id=0, has_side_effects=True, vmem_limit_bytes=56 * 2**20
+            collective_id=0, has_side_effects=True, vmem_limit_bytes=46 * 2**20
         ),
     )(
         counts,
@@ -672,6 +709,23 @@
         counts.reshape(1, BANDS),
         target.transpose(1, 0, 2),
     )
+    held = (
+        pltpu.VMEM((2, 2, TILES, 16, 128), bf16),
+        pltpu.VMEM((32, 2 * C), f32),
+        pltpu.VMEM((8, 128), f32),
+        pltpu.VMEM((2, BAND, LON, C), bf16),
+    )
+    results = pl.pallas_call(
+        back_kernel,
+        out_shape=held,
+        in_specs=[smem] + [vmem] * (1 + len(between)),
+        out_specs=(vmem,) * 4,
+        scratch_shapes=[pltpu.VMEM(shape, dtype) for shape, dtype in back_scratch]
+        + [pltpu.SemaphoreType.DMA((64,))] * 2,
+        compiler_params=pltpu.CompilerParams(
+            collective_id=1, has_side_effects=True, vmem_limit_bytes=28 * 2**20
+        ),
+    )(counts, conv_weight, *handed)
     grad_conv, grad_noise, band_loss, loss, grad_latent = pl.pallas_call(
         write_kernel,
         out_shape=(
@@ -684,7 +738,7 @@
         in_specs=[vmem] * 4,
         out_specs=(vmem,) * 4 + (anywhere,),
         scratch_shapes=[pltpu.VMEM((3 * KP, C), f32), pltpu.SemaphoreType.DMA((8,))],
-        compiler_params=pltpu.CompilerParams(vmem_limit_bytes=60 * 2**20),
+        compiler_params=pltpu.CompilerParams(vmem_limit_bytes=24 * 2**20),
     )(*results)
     return (loss.reshape(()), band_loss.reshape(BANDS), grad_conv, grad_noise, grad_latent)
 

time: 77.3 us -> 82.9 us (1.072)
  Pallas kernels: 76.5 us -> 82.1 us
    pallas_call x1 -> x2, Pallas kernels: 71.4 us -> 79.1 us  [the longest x1 43.8 us: per_device(): pl.pallas_call(back_kernel, out_shape=held, in_specs=[smem] + [vmem] * (1...]
    pallas_call x1, Pallas kernels: 5.14 us -> 2.93 us  [per_device(): pl.pallas_call(write_kernel, out_shape=(jax.ShapeDtypeStruct((9, V, C), f...]
where the time goes in v3:
time: 82.9 us; the launch traced here: 82.8 us
  Pallas kernels  82.1 us (99%)
    pallas_call x1, Pallas kernels, per_device(): pl.pallas_call(back_kernel, out_shape=held, in_specs=[smem] + [vmem] * (1...  43.8 us
    pallas_call x1, Pallas kernels, per_device(): pl.pallas_call(front_kernel, out_shape=[pltpu.VMEM(shape, dtype) for shap...  35.3 us
    pallas_call x1, Pallas kernels, per_device(): pl.pallas_call(write_kernel, out_shape=(jax.ShapeDtypeStruct((9, V, C), f...  2.93 us

profile of v3, /device:TPU:1, one launch (start us, length us, event | category | flops | bytes accessed | tf_op | source)
XLA Modules:
  0.0 82.8 jit_solution(13987585410366353731)
XLA Ops:
  0.6 0.0 copy-start.1
  0.6 0.0 copy-start
  0.7 35.3 %shard_map.110 = (f32[768,512]{1,0:T(8,128)S(1)}, bf16[6,2,256,256]{3,2,1,0:T(8,128)(2,1)S(1)}, f32[2,12,128,512]{3,2,1,0:T(8,128)S(1)}, f32[2,12,128,128]{3,2,1...) custom-call(s32[64]{0:T(128)} %counts.3, ...), custom_call_target="tpu_custom_call" | custom-call | tf_op jit(solution)/shard_map/pallas_call | solution.py:691
  36.0 0.0 copy-done.1
  36.0 0.0 copy-done
  36.0 43.8 %shard_map.111 = (bf16[2,2,48,16,128]{4,3,2,1,0:T(8,128)(2,1)S(1)}, f32[32,1024]{1,0:T(8,128)S(1)}, f32[8,128]{1,0:T(8,128)S(1)}, bf16[2,12,128,512]{3,2,1,0:T(8,128)(2,1)S(1)}) custom-call(s32[64]{0:T(128)S(1)} %copy-done.1, bf16[9,82,512]{2,1,0:T(8,128)(2,1)S(1)} %copy-done, f32[768,512]{1,0:T(8,128)S(1)} %get-tuple-element.24.payload, ...), custom_call_target="tpu_custom_call" | custom-call | tf_op jit(solution)/shard_map/pallas_call | solution.py:718
  79.8 2.9 %shard_map.112 = (f32[9,82,512]{2,1,0:T(8,128)}, f32[32,1024]{1,0:T(8,128)}, f32[1,64]{1,0:T(1,128)}, f32[1,1]{1,0:T(1,128)}, bf16[2,12,128,512]{3,2,1,0:T(8,128)(2,1)}) custom-call(bf16[2,2,48,16,128]{4,3,2,1,0:T(8,128)(2,1)S(1)} %get-tuple-element.34.full, f32[32,1024]{1,0:T(8,128)S(1)} %get-tuple-element.35.noise_in, ...), custom_call_target="tpu_custom_call" | custom-call | tf_op jit(solution)/shard_map/pallas_call | solution.py:729
Async XLA Ops:
  0.6 35.4 %copy-start.1 = (s32[64]{0:T(128)S(1)}, s32[64]{0:T(128)}, u32[]{:S(2)}) copy-start(s32[64]{0:T(128)} %counts.3) | copy-start | bytes 772
  0.6 35.4 %copy-start = (bf16[9,82,512]{2,1,0:T(8,128)(2,1)S(1)}, bf16[9,82,512]{2,1,0:T(8,128)(2,1)}, u32[]{:S(2)}) copy-start(bf16[9,82,512]{2,1,0:T(8,128)(2,1)} %conv_weight.3) | copy-start | bytes 2267140

commit v4 on v2

--- a/solution.py
+++ b/solution.py
@@ -12,6 +12,7 @@
 C, V, LON, BAND = 512, 82, 128, 12
 VP, KP = 88, 256
 PAIR = 2 * VP
+VA = 96
 BANDS = 64
 MESH = pl.DeviceIdType.MESH
 NX, NY, NZ = 4, 4, 8
@@ -97,12 +98,12 @@
 
 def kernel(
     counts, latent_hbm, conv_weight, noise_weight, noise_in, var_in, counts_in, target,
-    full, noise_out, band_out, latent_hbm_out,
-    latent, latent_out, weight, noise, var_weight, scale, norms, truth, modulation, edges, edge_prod, edge_send, edge_in, normed, inv_std, mixed,
+    full, noise_out, band_out, latent_out,
+    latent, forward_weight, weight, noise, var_weight, scale, norms, truth, modulation, edges, edge_prod, edge_send, edge_in, rows_beside, normed, inv_std, mixed,
     product, decoded, decoded_half, part_in, cross_in, coef, grads, grads_out, score,
-    grad_edge, grad_edge_in, stack, spread, turned, pack, payload, mixed_grad, small,
-    from_core, own, first, first_in, own2, second, second_in, over_z,
-    small_x, small_y, small_c, noises, send_sem, recv_sem, local_sem,
+    grad_edge, grad_edge_in, stack, spread, halo, turned, pack, payload, mixed_grad, small,
+    half, from_core, own, first, first_in, own2, second, second_in, over_z,
+    small_z, small_x, small_y, small_c, noises, send_sem, recv_sem, local_sem,
 ):
     f32, bf16 = jnp.float32, jnp.bfloat16
     place = Place()
@@ -123,11 +124,9 @@
         down = lax.broadcasted_iota(jnp.int32, (size, size), 0)
         return jnp.sum(jnp.where(across == down, row, 0), axis=1, keepdims=True)
 
-    for a in range(3):
-        for b in range(3):
-            pack[b * V : (b + 1) * V, :] = conv_weight[3 * a + b].astype(f32)
-        pack[3 * V :, :] = jnp.zeros((KP - 3 * V, C), f32)
-        weight[a * KP : (a + 1) * KP, :] = pack[...].astype(bf16)
+    for t in range(9):
+        forward_weight[t * VA + 80 : (t + 1) * VA, :] = jnp.zeros((VA - 80, C), bf16)
+        forward_weight[t * VA : t * VA + V, :] = conv_weight[t]
 
     var_total = jnp.sum(var_in[...], axis=1, keepdims=True)
     var_weight[...] = jnp.zeros_like(var_weight)
@@ -168,8 +167,8 @@
 
     def fold(ref, lanes):
         value = rolled(ref[0:VP, lanes], 1)
-        value = value + ref[V : V + VP, lanes]
-        return value + rolled(ref[2 * V : 2 * V + VP, lanes], -1)
+        value = value + ref[VA : VA + VP, lanes]
+        return value + rolled(ref[2 * VA : 2 * VA + VP, lanes], -1)
 
     load.wait()
 
@@ -196,10 +195,14 @@
     ]
     edge_copies = []
     for side, a, step in ((0, 2, -1), (1, 0, 1)):
-        edge_prod[...] = nt_dot(weight[a * KP : (a + 1) * KP, :], edges[side].reshape(2 * LON, C))
+        edge_prod[...] = nt_dot(forward_weight[3 * a * VA : 3 * (a + 1) * VA, :], edges[side].reshape(2 * LON, C))
         for i in range(2):
             edge_send[side, i] = fold(edge_prod, slice(i * LON, (i + 1) * LON))
         edge_copies.append(copies.send(edge_send.at[side], edge_in.at[side], place.band(step)))
+    row_copies = [
+        copies.send(edges.at[side], rows_beside.at[side], place.band(step))
+        for side, step in ((0, -1), (1, 1))
+    ]
 
     for i in range(2):
         mixed[i, 0] = jnp.zeros((LON, C), bf16)
@@ -227,7 +230,7 @@
                 value = None
                 for a in range(3):
                     rows_in = mixed[i, pl.ds(2 * pair + a, 2)].reshape(2 * LON, C)
-                    term = nt_dot(weight[a * KP : (a + 1) * KP, :], rows_in)
+                    term = nt_dot(forward_weight[3 * a * VA : 3 * (a + 1) * VA, :], rows_in)
                     value = term if value is None else value + term
                 product[i] = value
             if n == 0 and not mine:
@@ -260,18 +263,42 @@
         stack[slot, 2 * V + VP :, :] = jnp.zeros((KP - 2 * V - VP, LON), f32)
         return stack[slot].astype(bf16)
 
-    def weigh(pair):
+    core_copies = [None] * 3
+
+    def between_cores(a):
+        rows = pl.ds(pl.multiple_of(a * KP + (1 - core) * 128, 128), 128)
+        half[a] = payload[rows, :].astype(bf16)
+        core_copies[a] = copies.send(half.at[a], from_core.at[a], partner)
+
+    def weigh_edge(a):
+        left = []
+        for i in range(2):
+            if a == 0:
+                value = jnp.where(has_prev, spread[0, i, :, :LON], jnp.zeros((KP, LON), bf16))
+            else:
+                both = spread[lax.div(final, 2), i]
+                value = jnp.where(lax.rem(final, 2) == 1, both[:, LON:], both[:, :LON])
+                value = jnp.where(has_next, value, jnp.zeros((KP, LON), bf16))
+            left.append(value)
+        side = 1 if a == 0 else 0
+        return nn_dot(jnp.concatenate(left, axis=1), rows_beside[side].reshape(2 * LON, C))
+
+    def weigh(pair, last=False):
         for i in range(2):
             both = grads[pair, i].astype(f32)
             for r in range(2):
                 value = spread_row(both[r * VP : (r + 1) * VP], 2 * i + r)
-                spread[i, :, r * LON : (r + 1) * LON] = value
-                turned[i, 2 * pair + r + 1] = value.T
-        for a in range(3):
+                spread[pair, i, :, r * LON : (r + 1) * LON] = value
+        for a in TAP_ROWS:
             value = payload[a * KP : (a + 1) * KP, :]
             for i in range(2):
-                value = value + nn_dot(spread[i], mixed[i, pl.ds(2 * pair + a, 2)].reshape(2 * LON, C))
+                rows_in = mixed[i, pl.ds(2 * pair + a, 2)].reshape(2 * LON, C)
+                value = value + nn_dot(spread[pair, i], rows_in)
+            if last and a != 1:
+                value = value + weigh_edge(a)
             payload[a * KP : (a + 1) * KP, :] = value
+            if last:
+                between_cores(a)
 
     score[...] = jnp.zeros_like(score)
     payload[...] = jnp.zeros_like(payload)
@@ -346,35 +373,11 @@
         grad_edge[side] = stack[side, :PAIR].astype(bf16)
         grad_edge_copies.append(copies.send(grad_edge.at[side], grad_edge_in.at[side], place.band(step)))
 
-    weigh((1 - core) * 3 + 2)
-
-    core_copies = [None] * 3
-
-    def between_cores(s):
-        rows = pl.ds(pl.multiple_of(s * KP + (1 - core) * 128, 128), 128)
-        core_copies[s] = copies.send(payload.at[rows], from_core.at[s], partner)
-
-    between_cores(1)
-    for copy in grad_edge_copies:
+    for copy in row_copies:
         copy.wait_recv()
-    for side, a, there in ((1, 2, has_prev), (0, 0, has_next)):
-        both = jnp.where(there, grad_edge_in[side].astype(f32), 0.0)
-        values = [spread_row(both[i * VP : (i + 1) * VP], 2 * side + i) for i in range(2)]
-        payload[a * KP : (a + 1) * KP, :] += nn_dot(
-            jnp.concatenate(values, axis=1), edges[1 - side].reshape(2 * LON, C)
-        )
-        between_cores(a)
-        for i in range(2):
-            flipped = values[i].T
-            if side == 1:
-                turned[i, 0] = flipped
-            else:
-                turned[i, BAND + 1] = jnp.zeros_like(flipped)
-                for slot in range(2, BAND + 2):
-                    turned[i, slot] = jnp.where(count + 1 == slot, flipped, turned[i, slot])
+    weigh((1 - core) * 3 + 2, last=True)
 
     small[...] = jnp.zeros_like(small)
-    stores = []
 
     def points(i, r, row, part, gain_sum, shift_sum):
         lon = slice(part * 32, part * 32 + 32)
@@ -392,6 +395,17 @@
         latent_out[i, row, lon, :] = result.astype(bf16)
         return gain_sum, shift_sum
 
+    def turn():
+        for i in range(2):
+            turned[i, 0] = halo[1, i].T
+            trailing = halo[0, i].T
+            for pair in range(6):
+                for r in range(2):
+                    slot = 2 * pair + r + 1
+                    value = spread[pair, i, :, r * LON : (r + 1) * LON].T
+                    turned[i, slot] = jnp.where(count + 1 == slot, trailing, value)
+            turned[i, BAND + 1] = jnp.where(count == BAND, trailing, jnp.zeros_like(trailing))
+
     def backward(blocks):
         for block in blocks:
             i, pair = divmod(block, 6)
@@ -420,13 +434,6 @@
                 for q in range(4):
                     at = i * 8 + k + q
                     small[at : at + 1, :] += line[:, q * 128 : (q + 1) * 128]
-            store = pltpu.make_async_copy(
-                latent_out.at[i, 2 * pair : 2 * pair + 2],
-                latent_hbm_out.at[i, 2 * pair : 2 * pair + 2],
-                local_sem.at[1 + block],
-            )
-            store.start()
-            stores.append(store)
 
     def tile(ref, row, lane):
         return ref[pl.ds(pl.multiple_of(row, 16), 16), lane * 128 : (lane + 1) * 128]
@@ -438,7 +445,7 @@
             group = n * 8 + r
             for lane in range(4):
                 value = tile(payload, a * KP + core * 128 + r * 16, lane)
-                value = value + tile(from_core.at[a], r * 16, lane)
+                value = value + tile(from_core.at[a], r * 16, lane).astype(f32)
                 at = (group // 12, group % 12 * 4 + lane)
                 own[at] = value
                 first[at] = value.astype(bf16)
@@ -454,7 +461,20 @@
     stage1 = [scatter(0, first, first_in, 12, SETS[0][0])]
     take_from_core(2)
     stage1.append(scatter(1, first, first_in, 12, SETS[1][0]))
-    backward(range(0, 6))
+    for a in range(3):
+        for b in range(3):
+            pack[b * V : (b + 1) * V, :] = conv_weight[3 * a + b].astype(f32)
+        pack[3 * V :, :] = jnp.zeros((KP - 3 * V, C), f32)
+        weight[a * KP : (a + 1) * KP, :] = pack[...].astype(bf16)
+
+    for copy in grad_edge_copies:
+        copy.wait_recv()
+    for side, there in ((1, has_prev), (0, has_next)):
+        both = jnp.where(there, grad_edge_in[side].astype(f32), 0.0)
+        for i in range(2):
+            halo[side, i] = spread_row(both[i * VP : (i + 1) * VP], 2 * side + i)
+    turn()
+    backward(range(0, 3))
 
     stage2 = []
     for s in range(2):
@@ -468,7 +488,7 @@
             own2[s, t] = value
             second[s, t] = value.astype(bf16)
         stage2.append(scatter(s, second, second_in, 3, SETS[s][1]))
-    backward(range(6, 12))
+    backward(range(3, 6))
 
     for s in range(2):
         for copy in stage2[s]:
@@ -479,18 +499,21 @@
             for k in range(3):
                 value = value + second_in[s, k, t].astype(f32)
             over_z[place.z, s * 3 + t] = value.astype(bf16)
-    band = jnp.sum(jnp.sum(score[...], axis=1, keepdims=True), axis=0, keepdims=True)
-    lanes = lax.broadcasted_iota(jnp.int32, (1, 128), 1)
-    small[16:17, :] = jnp.where(lanes == place.lat, band, 0.0)
-    for t in range(2):
-        value = small[t * 16 : (t + 1) * 16, :]
-        coarse = value.astype(bf16)
-        over_z[place.z, 6 + t] = coarse
-        over_z[place.z, 8 + t] = (value - coarse.astype(f32)).astype(bf16)
     stage3 = [
         copies.send(over_z.at[place.z], over_z.at[place.z], device)
         for _, _, device in place.peers("z")
     ]
+    backward(range(6, 12))
+
+    band = jnp.sum(jnp.sum(score[...], axis=1, keepdims=True), axis=0, keepdims=True)
+    lanes = lax.broadcasted_iota(jnp.int32, (1, 128), 1)
+    small[16:17, :] = jnp.where(lanes == place.lat, band, 0.0)
+    small_z[place.z] = small[...]
+    small_copies = [
+        copies.send(small_z.at[place.z], small_z.at[place.z], device)
+        for _, _, device in place.peers("z")
+    ]
+
     for copy in stage3:
         copy.wait_recv()
 
@@ -509,16 +532,16 @@
                 value = value + over_z[z, s * 3 + t].astype(f32)
             full[core, s, piece(s) + t] = value.astype(bf16)
         stage4.append(gather(s, piece(s), 3, SETS[s][1]))
-    for t in range(2):
-        value = 0.0
-        for z in range(NZ):
-            value = value + (over_z[z, 6 + t].astype(f32) + over_z[z, 8 + t].astype(f32))
-        small_x[place.x, t * 16 : (t + 1) * 16, :] = value
+    for copy in small_copies:
+        copy.wait_recv()
+    total = small_z[0]
+    for z in range(1, NZ):
+        total = total + small_z[z]
+    small_x[place.x] = total
     small_copies = [
         copies.send(small_x.at[place.x], small_x.at[place.x], device)
         for _, _, device in place.peers("x")
     ]
-
     stage5 = []
     for s in range(2):
         for copy in stage4[s]:
@@ -561,8 +584,6 @@
 
     for copy in stage6:
         copy.wait_recv()
-    for store in stores:
-        store.wait()
     copies.finish()
 
 
@@ -599,7 +620,7 @@
     anywhere = pl.BlockSpec(memory_space=pl.ANY)
     scratch = [
         ((2, BAND, LON, C), bf16),
-        ((2, BAND, LON, C), bf16),
+        ((9 * VA, C), bf16),
         ((3 * KP, C), bf16),
         ((2, 32, 128), f32),
         ((VP, LON), f32),
@@ -608,13 +629,14 @@
         ((PAIR, LON), f32),
         ((2, 1, 2 * C), f32),
         ((2, 2, LON, C), bf16),
-        ((KP, 2 * LON), f32),
+        ((3 * VA, 2 * LON), f32),
         ((2, 2, VP, LON), f32),
         ((2, 2, VP, LON), f32),
+        ((2, 2, LON, C), bf16),
         ((2, BAND, LON, C), f32),
         ((2, BAND, LON, LON), f32),
         ((2, BAND + 2, LON, C), bf16),
-        ((2, KP, 2 * LON), f32),
+        ((2, 3 * VA, 2 * LON), f32),
         ((6, 2, PAIR, LON), f32),
         ((6, 2, PAIR, LON), bf16),
         ((3, 2, PAIR, LON), f32),
@@ -626,39 +648,42 @@
         ((2, PAIR, LON), bf16),
         ((2, PAIR, LON), bf16),
         ((4, KP, LON), f32),
-        ((2, KP, 2 * LON), bf16),
+        ((6, 2, KP, 2 * LON), bf16),
+        ((2, 2, KP, LON), bf16),
         ((2, BAND + 2, LON, KP), bf16),
         ((KP, C), f32),
         ((3 * KP, C), f32),
         ((2, LON, C), f32),
-        ((32, 128), f32),
-        ((3, 128, C), f32),
+        ((24, 128), f32),
+        ((3, 128, C), bf16),
+        ((3, 128, C), bf16),
         ((2, TILES, 16, 128), f32),
         ((2, TILES, 16, 128), bf16),
         ((2, 3, 12, 16, 128), bf16),
         ((2, 12, 16, 128), f32),
         ((2, 12, 16, 128), bf16),
         ((2, 3, 3, 16, 128), bf16),
-        ((NZ, 10, 16, 128), bf16),
-        ((4, 32, 128), f32),
-        ((4, 32, 128), f32),
-        ((2, 2, 32, 128), f32),
+        ((NZ, 6, 16, 128), bf16),
+        ((NZ, 24, 128), f32),
+        ((4, 24, 128), f32),
+        ((4, 24, 128), f32),
+        ((2, 2, 24, 128), f32),
         ((4, 2, 32, 128), f32),
     ]
     held = (
-        jax.ShapeDtypeStruct((2, 2, TILES, 16, 128), bf16),
-        jax.ShapeDtypeStruct((32, 2 * C), f32),
-        jax.ShapeDtypeStruct((8, 128), f32),
-        jax.ShapeDtypeStruct((2, BAND, LON, C), bf16),
+        pltpu.VMEM((2, 2, TILES, 16, 128), bf16),
+        pltpu.VMEM((32, 2 * C), f32),
+        pltpu.VMEM((8, 128), f32),
+        pltpu.VMEM((2, BAND, LON, C), bf16),
     )
     results = pl.pallas_call(
         kernel,
         out_shape=held,
         in_specs=[smem, anywhere] + [vmem] * 6,
-        out_specs=(vmem,) * 3 + (anywhere,),
+        out_specs=(vmem,) * 4,
         scratch_shapes=[pltpu.VMEM(shape, dtype) for shape, dtype in scratch]
         + [pltpu.SemaphoreType.DMA((SEMS,))] * 2
-        + [pltpu.SemaphoreType.DMA((16,))],
+        + [pltpu.SemaphoreType.DMA((1,))],
         compiler_params=pltpu.CompilerParams(
             collective_id=0, has_side_effects=True, vmem_limit_bytes=56 * 2**20
         ),
@@ -684,7 +709,7 @@
         in_specs=[vmem] * 4,
         out_specs=(vmem,) * 4 + (anywhere,),
         scratch_shapes=[pltpu.VMEM((3 * KP, C), f32), pltpu.SemaphoreType.DMA((8,))],
-        compiler_params=pltpu.CompilerParams(vmem_limit_bytes=60 * 2**20),
+        compiler_params=pltpu.CompilerParams(vmem_limit_bytes=24 * 2**20),
     )(*results)
     return (loss.reshape(()), band_loss.reshape(BANDS), grad_conv, grad_noise, grad_latent)
 

time: 77.3 us -> 71.5 us (0.925)
  Pallas kernels: 76.5 us -> 70.7 us
    pallas_call x1, Pallas kernels: 71.4 us -> 67.7 us  [per_device(): pl.pallas_call(kernel, out_shape=held, in_specs=[smem, anywhere] + [vmem]...]
    pallas_call x1, Pallas kernels: 5.14 us -> 2.93 us  [per_device(): pl.pallas_call(write_kernel, out_shape=(jax.ShapeDtypeStruct((9, V, C), f...]
where the time goes in v4:
time: 71.5 us; the launch traced here: 71.3 us
  Pallas kernels  70.7 us (99%)
    pallas_call x1, Pallas kernels, per_device(): pl.pallas_call(kernel, out_shape=held, in_specs=[smem, anywhere] + [vmem]...  67.7 us
    pallas_call x1, Pallas kernels, per_device(): pl.pallas_call(write_kernel, out_shape=(jax.ShapeDtypeStruct((9, V, C), f...  2.93 us

profile of v4, /device:TPU:1, one launch (start us, length us, event | category | flops | bytes accessed | tf_op | source)
XLA Modules:
  0.0 71.3 jit_solution(17990971999822495786)
XLA Ops:
  0.6 67.7 %shard_map.110 = (bf16[2,2,48,16,128]{4,3,2,1,0:T(8,128)(2,1)S(1)}, f32[32,1024]{1,0:T(8,128)S(1)}, f32[8,128]{1,0:T(8,128)S(1)}, bf16[2,12,128,512]{3,2,1,0:T(8,128)(2,1)S(1)}) custom-call(s32[64]{0:T(128)} %counts.1, bf16[2,12,128,512]{3,2,1,0:T(8,128)(2,1)} %latent_hbm.1, bf16[9,82,512]{2,1,0:T(8,128)(2,1)} %conv_weight.1, f32[32,1024]{1,0:T(8,128)} %noise_weight.1, ...), custom_call_target="tpu_custom_call" | custom-call | tf_op jit(solution)/shard_map/pallas_call | solution.py:679
  68.4 2.9 %shard_map.111 = (f32[9,82,512]{2,1,0:T(8,128)}, f32[32,1024]{1,0:T(8,128)}, f32[1,64]{1,0:T(1,128)}, f32[1,1]{1,0:T(1,128)}, bf16[2,12,128,512]{3,2,1,0:T(8,128)(2,1)}) custom-call(bf16[2,2,48,16,128]{4,3,2,1,0:T(8,128)(2,1)S(1)} %get-tuple-element.14.full, f32[32,1024]{1,0:T(8,128)S(1)} %get-tuple-element.15.noise_in, ...), custom_call_target="tpu_custom_call" | custom-call | tf_op jit(solution)/shard_map/pallas_call | solution.py:700

commit v5 on v4

--- a/solution.py
+++ b/solution.py
@@ -124,9 +124,65 @@
         down = lax.broadcasted_iota(jnp.int32, (size, size), 0)
         return jnp.sum(jnp.where(across == down, row, 0), axis=1, keepdims=True)
 
-    for t in range(9):
-        forward_weight[t * VA + 80 : (t + 1) * VA, :] = jnp.zeros((VA - 80, C), bf16)
-        forward_weight[t * VA : t * VA + V, :] = conv_weight[t]
+    for a in range(3):
+        for b in range(3):
+            lanes = slice(a * C, (a + 1) * C)
+            forward_weight[b * VA + 80 : (b + 1) * VA, lanes] = jnp.zeros((VA - 80, C), bf16)
+            forward_weight[b * VA : b * VA + V, lanes] = conv_weight[3 * a + b]
+
+    for i in range(2):
+        noise[i] = jnp.broadcast_to(column(noise_in[i : i + 1, :], 32), (32, 128))
+
+    for i in range(2):
+        for r in range(8):
+            part = noise_weight[:, r * 128 : (r + 1) * 128] * noise[i]
+            modulation[i, :, r * 128 : (r + 1) * 128] = jnp.sum(part, axis=0, keepdims=True)
+
+    def normalize(block):
+        widened = block.astype(f32)
+        average = jnp.sum(widened, axis=-1, keepdims=True) * (1.0 / C)
+        centred = widened - average
+        rate = lax.rsqrt(jnp.sum(centred * centred, axis=-1, keepdims=True) * (1.0 / C) + EPSILON)
+        return centred * rate, rate
+
+    def fold(ref, lanes):
+        value = rolled(ref[0:VP, lanes], 1)
+        value = value + ref[VA : VA + VP, lanes]
+        return value + rolled(ref[2 * VA : 2 * VA + VP, lanes], -1)
+
+    load.wait()
+
+    def normalize_modulate(i, row, lon, gain, shift):
+        value, rate = normalize(latent[i, row, lon, :])
+        return value, rate, (value * gain + shift).astype(bf16)
+
+    def edge_rows(n, carry):
+        lon = pl.ds(pl.multiple_of(n * 32, 32), 32)
+        for side, row in ((0, 0), (1, final)):
+            for i in range(2):
+                _, _, value = normalize_modulate(
+                    i, row, lon, 1.0 + modulation[i, :, :C], modulation[i, :, C:]
+                )
+                edges[side, i, lon, :] = value
+        return carry
+
+    lax.fori_loop(0, 4, edge_rows, 0)
+    greeted()
+    noises[place.member] = noise[...]
+    noise_copies = [
+        copies.send(noises.at[place.member], noises.at[place.member], device)
+        for device in (partner, place.at(y=beside), place.at(y=beside, core=1 - core))
+    ]
+    edge_copies = []
+    for side, a, step in ((0, 2, -1), (1, 0, 1)):
+        edge_prod[...] = nt_dot(forward_weight[:, a * C : (a + 1) * C], edges[side].reshape(2 * LON, C))
+        for i in range(2):
+            edge_send[side, i] = fold(edge_prod, slice(i * LON, (i + 1) * LON))
+        edge_copies.append(copies.send(edge_send.at[side], edge_in.at[side], place.band(step)))
+    row_copies = [
+        copies.send(edges.at[side], rows_beside.at[side], place.band(step))
+        for side, step in ((0, -1), (1, 1))
+    ]
 
     var_total = jnp.sum(var_in[...], axis=1, keepdims=True)
     var_weight[...] = jnp.zeros_like(var_weight)
@@ -151,60 +207,6 @@
     )
     truth[...] = jnp.zeros_like(truth)
     for i in range(2):
-        noise[i] = jnp.broadcast_to(column(noise_in[i : i + 1, :], 32), (32, 128))
-
-    for i in range(2):
-        for r in range(8):
-            part = noise_weight[:, r * 128 : (r + 1) * 128] * noise[i]
-            modulation[i, :, r * 128 : (r + 1) * 128] = jnp.sum(part, axis=0, keepdims=True)
-
-    def normalize(block):
-        widened = block.astype(f32)
-        average = jnp.sum(widened, axis=-1, keepdims=True) * (1.0 / C)
-        centred = widened - average
-        rate = lax.rsqrt(jnp.sum(centred * centred, axis=-1, keepdims=True) * (1.0 / C) + EPSILON)
-        return centred * rate, rate
-
-    def fold(ref, lanes):
-        value = rolled(ref[0:VP, lanes], 1)
-        value = value + ref[VA : VA + VP, lanes]
-        return value + rolled(ref[2 * VA : 2 * VA + VP, lanes], -1)
-
-    load.wait()
-
-    def normalize_modulate(i, row, lon, gain, shift):
-        value, rate = normalize(latent[i, row, lon, :])
-        return value, rate, (value * gain + shift).astype(bf16)
-
-    def edge_rows(n, carry):
-        lon = pl.ds(pl.multiple_of(n * 32, 32), 32)
-        for side, row in ((0, 0), (1, final)):
-            for i in range(2):
-                _, _, value = normalize_modulate(
-                    i, row, lon, 1.0 + modulation[i, :, :C], modulation[i, :, C:]
-                )
-                edges[side, i, lon, :] = value
-        return carry
-
-    lax.fori_loop(0, 4, edge_rows, 0)
-    greeted()
-    noises[place.member] = noise[...]
-    noise_copies = [
-        copies.send(noises.at[place.member], noises.at[place.member], device)
-        for device in (partner, place.at(y=beside), place.at(y=beside, core=1 - core))
-    ]
-    edge_copies = []
-    for side, a, step in ((0, 2, -1), (1, 0, 1)):
-        edge_prod[...] = nt_dot(forward_weight[3 * a * VA : 3 * (a + 1) * VA, :], edges[side].reshape(2 * LON, C))
-        for i in range(2):
-            edge_send[side, i] = fold(edge_prod, slice(i * LON, (i + 1) * LON))
-        edge_copies.append(copies.send(edge_send.at[side], edge_in.at[side], place.band(step)))
-    row_copies = [
-        copies.send(edges.at[side], rows_beside.at[side], place.band(step))
-        for side, step in ((0, -1), (1, 1))
-    ]
-
-    for i in range(2):
         mixed[i, 0] = jnp.zeros((LON, C), bf16)
         mixed[i, BAND + 1] = jnp.zeros((LON, C), bf16)
 
@@ -227,12 +229,10 @@
         for mine in (False, True):
             pair = (core if mine else 1 - core) * 3 + n
             for i in range(2):
-                value = None
-                for a in range(3):
-                    rows_in = mixed[i, pl.ds(2 * pair + a, 2)].reshape(2 * LON, C)
-                    term = nt_dot(forward_weight[3 * a * VA : 3 * (a + 1) * VA, :], rows_in)
-                    value = term if value is None else value + term
-                product[i] = value
+                rows_in = jnp.concatenate(
+                    [mixed[i, pl.ds(2 * pair + a, 2)].reshape(2 * LON, C) for a in range(3)], axis=1
+                )
+                product[i] = nt_dot(forward_weight[...], rows_in)
             if n == 0 and not mine:
                 for copy in edge_copies:
                     copy.wait_recv()
@@ -283,17 +283,19 @@
         side = 1 if a == 0 else 0
         return nn_dot(jnp.concatenate(left, axis=1), rows_beside[side].reshape(2 * LON, C))
 
-    def weigh(pair, last=False):
+    def weigh(pair, begin=False, last=False):
         for i in range(2):
             both = grads[pair, i].astype(f32)
             for r in range(2):
                 value = spread_row(both[r * VP : (r + 1) * VP], 2 * i + r)
                 spread[pair, i, :, r * LON : (r + 1) * LON] = value
         for a in TAP_ROWS:
-            value = payload[a * KP : (a + 1) * KP, :]
-            for i in range(2):
-                rows_in = mixed[i, pl.ds(2 * pair + a, 2)].reshape(2 * LON, C)
-                value = value + nn_dot(spread[pair, i], rows_in)
+            rows_in = jnp.concatenate(
+                [mixed[i, pl.ds(2 * pair + a, 2)].reshape(2 * LON, C) for i in range(2)], axis=0
+            )
+            value = nn_dot(jnp.concatenate([spread[pair, 0], spread[pair, 1]], axis=1), rows_in)
+            if not begin:
+                value = value + payload[a * KP : (a + 1) * KP, :]
             if last and a != 1:
                 value = value + weigh_edge(a)
             payload[a * KP : (a + 1) * KP, :] = value
@@ -301,7 +303,6 @@
                 between_cores(a)
 
     score[...] = jnp.zeros_like(score)
-    payload[...] = jnp.zeros_like(payload)
     grad_copies = []
     for n in range(3):
         pair = core * 3 + n
@@ -356,7 +357,7 @@
 
         lax.fori_loop(0, PAIR // 16, crps, 0)
         grad_copies.append(copies.send(grads_out.at[n], grads.at[pair], partner))
-        weigh(pair)
+        weigh(pair, begin=n == 0)
         if n > 0:
             grad_copies[n - 1].wait_recv()
             weigh((1 - core) * 3 + n - 1)
@@ -409,11 +410,14 @@
     def backward(blocks):
         for block in blocks:
             i, pair = divmod(block, 6)
-            value = None
-            for a in range(3):
-                left = turned[i, 2 * pair + 2 - a : 2 * pair + 4 - a].reshape(2 * LON, KP)
-                term = nn_dot(left, weight[a * KP : (a + 1) * KP, :])
-                value = term if value is None else value + term
+            left = jnp.concatenate(
+                [
+                    turned[i, 2 * pair + 2 - a : 2 * pair + 4 - a].reshape(2 * LON, KP)
+                    for a in range(3)
+                ],
+                axis=1,
+            )
+            value = nn_dot(left, weight[...])
             mixed_grad[...] = value.reshape(2, LON, C)
 
             zero = jnp.zeros((8, C), f32)
@@ -587,7 +591,7 @@
     copies.finish()
 
 
-def write_kernel(full, noise_in, band_in, latent_in, conv_out, noise_out, band_out, loss_out, latent_out, flat, sem):
+def write_kernel(full, noise_in, band_in, latent_in, conv_out, noise_out, band_out, loss_out, latent_out, flat, conv, sem):
     moves = []
     for i in range(2):
         for part in range(4):
@@ -605,7 +609,10 @@
                 flat[row : row + 16, lanes] = full[c, s, t].astype(jnp.float32)
     for a in range(3):
         for b in range(3):
-            conv_out[3 * a + b] = flat[a * KP + b * V : a * KP + b * V + V, :]
+            t = 3 * a + b
+            conv[t] = flat[a * KP + b * V : a * KP + b * V + V, :]
+            moves.append(pltpu.make_async_copy(conv.at[t], conv_out.at[t], sem.at[8 + t]))
+            moves[-1].start()
     noise_out[...] = noise_in[...]
     band_out[...] = band_in[0:1, 0:BANDS]
     loss_out[...] = band_in[1:2, 0:1]
@@ -620,7 +627,7 @@
     anywhere = pl.BlockSpec(memory_space=pl.ANY)
     scratch = [
         ((2, BAND, LON, C), bf16),
-        ((9 * VA, C), bf16),
+        ((3 * VA, 3 * C), bf16),
         ((3 * KP, C), bf16),
         ((2, 32, 128), f32),
         ((VP, LON), f32),
@@ -707,8 +714,12 @@
             jax.ShapeDtypeStruct((2, BAND, LON, C), bf16),
         ),
         in_specs=[vmem] * 4,
-        out_specs=(vmem,) * 4 + (anywhere,),
-        scratch_shapes=[pltpu.VMEM((3 * KP, C), f32), pltpu.SemaphoreType.DMA((8,))],
+        out_specs=(anywhere,) + (vmem,) * 3 + (anywhere,),
+        scratch_shapes=[
+            pltpu.VMEM((3 * KP, C), f32),
+            pltpu.VMEM((9, V, C), f32),
+            pltpu.SemaphoreType.DMA((17,)),
+        ],
         compiler_params=pltpu.CompilerParams(vmem_limit_bytes=24 * 2**20),
     )(*results)
     return (loss.reshape(()), band_loss.reshape(BANDS), grad_conv, grad_noise, grad_latent)

time: 71.5 us -> 71.5 us (level)
  no operation moved by 1% of the time
where the time goes in v5:
time: 71.5 us; the launch traced here: 71.4 us
  Pallas kernels  70.7 us (99%)
    pallas_call x1, Pallas kernels, per_device(): pl.pallas_call(kernel, out_shape=held, in_specs=[smem, anywhere] + [vmem]...  67.7 us
    pallas_call x1, Pallas kernels, per_device(): pl.pallas_call(write_kernel, out_shape=(jax.ShapeDtypeStruct((9, V, C), f...  2.98 us

profile of v5, /device:TPU:1, one launch (start us, length us, event | category | flops | bytes accessed | tf_op | source)
XLA Modules:
  0.0 71.4 jit_solution(900768895082387537)
XLA Ops:
  0.6 67.7 %shard_map.110 = (bf16[2,2,48,16,128]{4,3,2,1,0:T(8,128)(2,1)S(1)}, f32[32,1024]{1,0:T(8,128)S(1)}, f32[8,128]{1,0:T(8,128)S(1)}, bf16[2,12,128,512]{3,2,1,0:T(8,128)(2,1)S(1)}) custom-call(s32[64]{0:T(128)} %counts.1, bf16[2,12,128,512]{3,2,1,0:T(8,128)(2,1)} %latent_hbm.1, bf16[9,82,512]{2,1,0:T(8,128)(2,1)} %conv_weight.1, f32[32,1024]{1,0:T(8,128)} %noise_weight.1, ...), custom_call_target="tpu_custom_call" | custom-call | tf_op jit(solution)/shard_map/pallas_call | solution.py:686
  68.4 3.0 %shard_map.111 = (f32[9,82,512]{2,1,0:T(8,128)}, f32[32,1024]{1,0:T(8,128)}, f32[1,64]{1,0:T(1,128)}, f32[1,1]{1,0:T(1,128)}, bf16[2,12,128,512]{3,2,1,0:T(8,128)(2,1)}) custom-call(bf16[2,2,48,16,128]{4,3,2,1,0:T(8,128)(2,1)S(1)} %get-tuple-element.14.full, f32[32,1024]{1,0:T(8,128)S(1)} %get-tuple-element.15.noise_in, ...), custom_call_target="tpu_custom_call" | custom-call | tf_op jit(solution)/shard_map/pallas_call | solution.py:707

commit v6 on v5

--- a/solution.py
+++ b/solution.py
@@ -97,9 +97,9 @@
 
 
 def kernel(
-    counts, latent_hbm, conv_weight, noise_weight, noise_in, var_in, counts_in, target,
+    counts, latent_hbm, conv_hbm, noise_weight_hbm, noise_hbm, var_hbm, counts_hbm, target_hbm,
     full, noise_out, band_out, latent_out,
-    latent, forward_weight, weight, noise, var_weight, scale, norms, truth, modulation, edges, edge_prod, edge_send, edge_in, rows_beside, normed, inv_std, mixed,
+    latent, conv_weight, noise_weight, noise_in, var_in, counts_in, target, forward_weight, weight, noise, var_weight, scale, norms, truth, modulation, edges, edge_prod, edge_send, edge_in, rows_beside, normed, inv_std, mixed,
     product, decoded, decoded_half, part_in, cross_in, coef, grads, grads_out, score,
     grad_edge, grad_edge_in, stack, spread, halo, turned, pack, payload, mixed_grad, small,
     half, from_core, own, first, first_in, own2, second, second_in, over_z,
@@ -108,9 +108,21 @@
     f32, bf16 = jnp.float32, jnp.bfloat16
     place = Place()
     copies = Copies(send_sem, recv_sem)
+    loads = [
+        pltpu.make_async_copy(src, dst, local_sem.at[n])
+        for n, (src, dst) in enumerate((
+            (noise_hbm, noise_in),
+            (noise_weight_hbm, noise_weight),
+            (conv_hbm, conv_weight),
+            (latent_hbm, latent),
+            (var_hbm, var_in),
+            (counts_hbm, counts_in),
+            (target_hbm, target),
+        ))
+    ]
+    for load in loads:
+        load.start()
     greeted = greet(place)
-    load = pltpu.make_async_copy(latent_hbm, latent, local_sem.at[0])
-    load.start()
     count = counts[place.lat]
     final = jnp.maximum(count - 1, 0)
     core = place.core
@@ -124,12 +136,8 @@
         down = lax.broadcasted_iota(jnp.int32, (size, size), 0)
         return jnp.sum(jnp.where(across == down, row, 0), axis=1, keepdims=True)
 
-    for a in range(3):
-        for b in range(3):
-            lanes = slice(a * C, (a + 1) * C)
-            forward_weight[b * VA + 80 : (b + 1) * VA, lanes] = jnp.zeros((VA - 80, C), bf16)
-            forward_weight[b * VA : b * VA + V, lanes] = conv_weight[3 * a + b]
-
+    for load in loads[:2]:
+        load.wait()
     for i in range(2):
         noise[i] = jnp.broadcast_to(column(noise_in[i : i + 1, :], 32), (32, 128))
 
@@ -150,7 +158,14 @@
         value = value + ref[VA : VA + VP, lanes]
         return value + rolled(ref[2 * VA : 2 * VA + VP, lanes], -1)
 
-    load.wait()
+    loads[2].wait()
+    for a in range(3):
+        for b in range(3):
+            lanes = slice(a * C, (a + 1) * C)
+            forward_weight[b * VA + 80 : (b + 1) * VA, lanes] = jnp.zeros((VA - 80, C), bf16)
+            forward_weight[b * VA : b * VA + V, lanes] = conv_weight[3 * a + b]
+
+    loads[3].wait()
 
     def normalize_modulate(i, row, lon, gain, shift):
         value, rate = normalize(latent[i, row, lon, :])
@@ -166,23 +181,27 @@
                 edges[side, i, lon, :] = value
         return carry
 
-    lax.fori_loop(0, 4, edge_rows, 0)
+    lax.fori_loop(0, 4, edge_rows, 0, unroll=2)
     greeted()
+    edge_copies = []
+    for side, a, step in ((0, 2, -1), (1, 0, 1)):
+        edge_prod[...] = nt_dot(forward_weight[:, a * C : (a + 1) * C], edges[side].reshape(2 * LON, C))
+        for i in range(2):
+            value = fold(edge_prod, slice(i * LON, (i + 1) * LON))
+            edge_send[side, i * VP : (i + 1) * VP, :] = value.astype(bf16)
+        edge_copies.append(copies.send(edge_send.at[side], edge_in.at[side], place.band(step)))
+    row_copies = [
+        copies.send(edges.at[side], rows_beside.at[side], place.band(step))
+        for side, step in ((0, -1), (1, 1))
+    ]
+
     noises[place.member] = noise[...]
     noise_copies = [
         copies.send(noises.at[place.member], noises.at[place.member], device)
         for device in (partner, place.at(y=beside), place.at(y=beside, core=1 - core))
     ]
-    edge_copies = []
-    for side, a, step in ((0, 2, -1), (1, 0, 1)):
-        edge_prod[...] = nt_dot(forward_weight[:, a * C : (a + 1) * C], edges[side].reshape(2 * LON, C))
-        for i in range(2):
-            edge_send[side, i] = fold(edge_prod, slice(i * LON, (i + 1) * LON))
-        edge_copies.append(copies.send(edge_send.at[side], edge_in.at[side], place.band(step)))
-    row_copies = [
-        copies.send(edges.at[side], rows_beside.at[side], place.band(step))
-        for side, step in ((0, -1), (1, 1))
-    ]
+    for load in loads[4:]:
+        load.wait()
 
     var_total = jnp.sum(var_in[...], axis=1, keepdims=True)
     var_weight[...] = jnp.zeros_like(var_weight)
@@ -224,9 +243,13 @@
 
     part_copies, same_copies, other_copies = [], [], []
     for n in range(3):
-        for begin, end in (((0, 3), (5, 9)), ((3, 5), (9, 11)), ((11, 12),))[n]:
-            lax.fori_loop(begin, end, normalize_row, 0)
         for mine in (False, True):
+            if n == 0:
+                half_start = 5 * (core if mine else 1 - core)
+                lax.fori_loop(half_start, half_start + 4, normalize_row, 0)
+            elif not mine:
+                for row in ((4, 9, 10), (11,))[n - 1]:
+                    normalize_row(row, 0)
             pair = (core if mine else 1 - core) * 3 + n
             for i in range(2):
                 rows_in = jnp.concatenate(
@@ -236,12 +259,13 @@
             if n == 0 and not mine:
                 for copy in edge_copies:
                     copy.wait_recv()
+            beside_rows = [edge_in[side].astype(f32).reshape(2, VP, LON) for side in range(2)]
             for i in range(2):
                 for r in range(2):
                     row = 2 * pair + r
                     value = fold(product.at[i], slice(r * LON, (r + 1) * LON))
-                    value = value + jnp.where((row == 0) & has_prev, edge_in[1, i], 0.0)
-                    value = value + jnp.where((row == final) & has_next, edge_in[0, i], 0.0)
+                    value = value + jnp.where((row == 0) & has_prev, beside_rows[1][i], 0.0)
+                    value = value + jnp.where((row == final) & has_next, beside_rows[0][i], 0.0)
                     decoded[pair, i, r * VP : (r + 1) * VP, :] = value
                 decoded_half[pair, i] = decoded[pair, i].astype(bf16)
             if mine:
@@ -309,6 +333,9 @@
         for r in range(2):
             coef[r * VP : (r + 1) * VP, :] = var_weight[...] * scale[pl.ds(2 * pair + r, 1), :]
             truth[r * VP : r * VP + V, :] = target[2 * pair + r].astype(f32)
+        if n > 0:
+            grad_copies[n - 1].wait_recv()
+            weigh((1 - core) * 3 + n - 1)
         part_copies[n].wait_recv()
         same_copies[n].wait_recv()
         other_copies[n].wait_recv()
@@ -358,9 +385,6 @@
         lax.fori_loop(0, PAIR // 16, crps, 0)
         grad_copies.append(copies.send(grads_out.at[n], grads.at[pair], partner))
         weigh(pair, begin=n == 0)
-        if n > 0:
-            grad_copies[n - 1].wait_recv()
-            weigh((1 - core) * 3 + n - 1)
     grad_copies[2].wait_recv()
 
     for i in range(2):
@@ -627,6 +651,12 @@
     anywhere = pl.BlockSpec(memory_space=pl.ANY)
     scratch = [
         ((2, BAND, LON, C), bf16),
+        ((9, V, C), bf16),
+        ((32, 2 * C), f32),
+        ((2, 32), f32),
+        ((1, V), f32),
+        ((1, BANDS), jnp.int32),
+        ((BAND, V, LON), bf16),
         ((3 * VA, 3 * C), bf16),
         ((3 * KP, C), bf16),
         ((2, 32, 128), f32),
@@ -637,8 +667,8 @@
         ((2, 1, 2 * C), f32),
         ((2, 2, LON, C), bf16),
         ((3 * VA, 2 * LON), f32),
-        ((2, 2, VP, LON), f32),
-        ((2, 2, VP, LON), f32),
+        ((2, PAIR, LON), bf16),
+        ((2, PAIR, LON), bf16),
         ((2, 2, LON, C), bf16),
         ((2, BAND, LON, C), f32),
         ((2, BAND, LON, LON), f32),
@@ -686,11 +716,11 @@
     results = pl.pallas_call(
         kernel,
         out_shape=held,
-        in_specs=[smem, anywhere] + [vmem] * 6,
+        in_specs=[smem] + [anywhere] * 7,
         out_specs=(vmem,) * 4,
         scratch_shapes=[pltpu.VMEM(shape, dtype) for shape, dtype in scratch]
         + [pltpu.SemaphoreType.DMA((SEMS,))] * 2
-        + [pltpu.SemaphoreType.DMA((1,))],
+        + [pltpu.SemaphoreType.DMA((7,))],
         compiler_params=pltpu.CompilerParams(
             collective_id=0, has_side_effects=True, vmem_limit_bytes=56 * 2**20
         ),

time: 71.5 us -> 69.9 us (0.978)
  Pallas kernels: 70.7 us -> 69.2 us
    pallas_call x1, Pallas kernels: 67.7 us -> 66.2 us  [per_device(): pl.pallas_call(kernel, out_shape=held, in_specs=[smem] + [anywhere] * 7,...]
where the time goes in v6:
time: 69.9 us; the launch traced here: 69.8 us
  Pallas kernels  69.2 us (99%)
    pallas_call x1, Pallas kernels, per_device(): pl.pallas_call(kernel, out_shape=held, in_specs=[smem] + [anywhere] * 7,...  66.2 us
    pallas_call x1, Pallas kernels, per_device(): pl.pallas_call(write_kernel, out_shape=(jax.ShapeDtypeStruct((9, V, C), f...  2.98 us

profile of v6, /device:TPU:1, one launch (start us, length us, event | category | flops | bytes accessed | tf_op | source)
XLA Modules:
  0.0 69.8 jit_solution(14178154781171145515)
XLA Ops:
  0.6 66.2 %shard_map.110 = (bf16[2,2,48,16,128]{4,3,2,1,0:T(8,128)(2,1)S(1)}, f32[32,1024]{1,0:T(8,128)S(1)}, f32[8,128]{1,0:T(8,128)S(1)}, bf16[2,12,128,512]{3,2,1,0:T(8,128)(2,1)S(1)}) custom-call(s32[64]{0:T(128)} %counts.1, bf16[2,12,128,512]{3,2,1,0:T(8,128)(2,1)} %latent_hbm.1, bf16[9,82,512]{2,1,0:T(8,128)(2,1)} %conv_hbm.1, f32[32,1024]{1,0:T(8,128)} %noise_weight_hbm.1, ...), custom_call_target="tpu_custom_call" | custom-call | tf_op jit(solution)/shard_map/pallas_call | solution.py:716
  66.8 3.0 %shard_map.111 = (f32[9,82,512]{2,1,0:T(8,128)}, f32[32,1024]{1,0:T(8,128)}, f32[1,64]{1,0:T(1,128)}, f32[1,1]{1,0:T(1,128)}, bf16[2,12,128,512]{3,2,1,0:T(8,128)(2,1)}) custom-call(bf16[2,2,48,16,128]{4,3,2,1,0:T(8,128)(2,1)S(1)} %get-tuple-element.14.full, f32[32,1024]{1,0:T(8,128)S(1)} %get-tuple-element.15.noise_in, ...), custom_call_target="tpu_custom_call" | custom-call | tf_op jit(solution)/shard_map/pallas_call | solution.py:737

commit v7 on v6

--- a/solution.py
+++ b/solution.py
@@ -39,7 +39,7 @@
     def peers(self, axis):
         count = {"x": NX, "y": NY, "z": NZ, "core": 2}[axis]
         mine = getattr(self, axis)
-        for k in range(1, count):
+        for k in sorted(range(1, count), key=lambda k: -min(k, count - k)):
             there = lax.rem(mine + k, count)
             yield k, there, self.at(**{axis: there})
 
@@ -188,7 +188,7 @@
         edge_prod[...] = nt_dot(forward_weight[:, a * C : (a + 1) * C], edges[side].reshape(2 * LON, C))
         for i in range(2):
             value = fold(edge_prod, slice(i * LON, (i + 1) * LON))
-            edge_send[side, i * VP : (i + 1) * VP, :] = value.astype(bf16)
+            edge_send[side, i * VP : (i + 1) * VP, :] = value
         edge_copies.append(copies.send(edge_send.at[side], edge_in.at[side], place.band(step)))
     row_copies = [
         copies.send(edges.at[side], rows_beside.at[side], place.band(step))
@@ -259,7 +259,7 @@
             if n == 0 and not mine:
                 for copy in edge_copies:
                     copy.wait_recv()
-            beside_rows = [edge_in[side].astype(f32).reshape(2, VP, LON) for side in range(2)]
+            beside_rows = [edge_in[side].reshape(2, VP, LON) for side in range(2)]
             for i in range(2):
                 for r in range(2):
                     row = 2 * pair + r
@@ -326,6 +326,19 @@
             if last:
                 between_cores(a)
 
+    def turn(pair):
+        for i in range(2):
+            for r in range(2):
+                turned[i, 2 * pair + r + 1] = spread[pair, i, :, r * LON : (r + 1) * LON].T
+
+    def turn_halo():
+        for i in range(2):
+            turned[i, 0] = halo[1, i].T
+            trailing = halo[0, i].T
+            turned[i, BAND + 1] = jnp.where(count == BAND, trailing, jnp.zeros_like(trailing))
+            for slot in range(2, BAND + 1):
+                turned[i, slot] = jnp.where(count + 1 == slot, trailing, turned[i, slot])
+
     score[...] = jnp.zeros_like(score)
     grad_copies = []
     for n in range(3):
@@ -336,6 +349,15 @@
         if n > 0:
             grad_copies[n - 1].wait_recv()
             weigh((1 - core) * 3 + n - 1)
+        if n == 2:
+            for a in range(3):
+                for b in range(3):
+                    pack[b * V : (b + 1) * V, :] = conv_weight[3 * a + b].astype(f32)
+                pack[3 * V :, :] = jnp.zeros((KP - 3 * V, C), f32)
+                weight[a * KP : (a + 1) * KP, :] = pack[...].astype(bf16)
+            for m in range(2):
+                turn(core * 3 + m)
+                turn((1 - core) * 3 + m)
         part_copies[n].wait_recv()
         same_copies[n].wait_recv()
         other_copies[n].wait_recv()
@@ -420,17 +442,6 @@
         latent_out[i, row, lon, :] = result.astype(bf16)
         return gain_sum, shift_sum
 
-    def turn():
-        for i in range(2):
-            turned[i, 0] = halo[1, i].T
-            trailing = halo[0, i].T
-            for pair in range(6):
-                for r in range(2):
-                    slot = 2 * pair + r + 1
-                    value = spread[pair, i, :, r * LON : (r + 1) * LON].T
-                    turned[i, slot] = jnp.where(count + 1 == slot, trailing, value)
-            turned[i, BAND + 1] = jnp.where(count == BAND, trailing, jnp.zeros_like(trailing))
-
     def backward(blocks):
         for block in blocks:
             i, pair = divmod(block, 6)
@@ -489,20 +500,16 @@
     stage1 = [scatter(0, first, first_in, 12, SETS[0][0])]
     take_from_core(2)
     stage1.append(scatter(1, first, first_in, 12, SETS[1][0]))
-    for a in range(3):
-        for b in range(3):
-            pack[b * V : (b + 1) * V, :] = conv_weight[3 * a + b].astype(f32)
-        pack[3 * V :, :] = jnp.zeros((KP - 3 * V, C), f32)
-        weight[a * KP : (a + 1) * KP, :] = pack[...].astype(bf16)
-
     for copy in grad_edge_copies:
         copy.wait_recv()
     for side, there in ((1, has_prev), (0, has_next)):
         both = jnp.where(there, grad_edge_in[side].astype(f32), 0.0)
         for i in range(2):
             halo[side, i] = spread_row(both[i * VP : (i + 1) * VP], 2 * side + i)
-    turn()
-    backward(range(0, 3))
+    turn(core * 3 + 2)
+    turn((1 - core) * 3 + 2)
+    turn_halo()
+    backward(range(0, 4))
 
     stage2 = []
     for s in range(2):
@@ -516,7 +523,7 @@
             own2[s, t] = value
             second[s, t] = value.astype(bf16)
         stage2.append(scatter(s, second, second_in, 3, SETS[s][1]))
-    backward(range(3, 6))
+    backward(range(4, 7))
 
     for s in range(2):
         for copy in stage2[s]:
@@ -531,7 +538,7 @@
         copies.send(over_z.at[place.z], over_z.at[place.z], device)
         for _, _, device in place.peers("z")
     ]
-    backward(range(6, 12))
+    backward(range(7, 12))
 
     band = jnp.sum(jnp.sum(score[...], axis=1, keepdims=True), axis=0, keepdims=True)
     lanes = lax.broadcasted_iota(jnp.int32, (1, 128), 1)
@@ -667,8 +674,8 @@
         ((2, 1, 2 * C), f32),
         ((2, 2, LON, C), bf16),
         ((3 * VA, 2 * LON), f32),
-        ((2, PAIR, LON), bf16),
-        ((2, PAIR, LON), bf16),
+        ((2, PAIR, LON), f32),
+        ((2, PAIR, LON), f32),
         ((2, 2, LON, C), bf16),
         ((2, BAND, LON, C), f32),
         ((2, BAND, LON, LON), f32),

time: 69.9 us -> 70.8 us (1.013)
  Pallas kernels: 69.2 us -> 70 us
    pallas_call x1, Pallas kernels: 66.2 us -> 67 us  [per_device(): pl.pallas_call(kernel, out_shape=held, in_specs=[smem] + [anywhere] * 7,...]
where the time goes in v7:
time: 70.8 us; the launch traced here: 70.7 us
  Pallas kernels  70 us (99%)
    pallas_call x1, Pallas kernels, per_device(): pl.pallas_call(kernel, out_shape=held, in_specs=[smem] + [anywhere] * 7,...  67 us
    pallas_call x1, Pallas kernels, per_device(): pl.pallas_call(write_kernel, out_shape=(jax.ShapeDtypeStruct((9, V, C), f...  2.98 us

profile of v7, /device:TPU:1, one launch (start us, length us, event | category | flops | bytes accessed | tf_op | source)
XLA Modules:
  0.0 70.7 jit_solution(1829940824063882055)
XLA Ops:
  0.6 67.0 %shard_map.110 = (bf16[2,2,48,16,128]{4,3,2,1,0:T(8,128)(2,1)S(1)}, f32[32,1024]{1,0:T(8,128)S(1)}, f32[8,128]{1,0:T(8,128)S(1)}, bf16[2,12,128,512]{3,2,1,0:T(8,128)(2,1)S(1)}) custom-call(s32[64]{0:T(128)} %counts.1, bf16[2,12,128,512]{3,2,1,0:T(8,128)(2,1)} %latent_hbm.1, bf16[9,82,512]{2,1,0:T(8,128)(2,1)} %conv_hbm.1, f32[32,1024]{1,0:T(8,128)} %noise_weight_hbm.1, ...), custom_call_target="tpu_custom_call" | custom-call | tf_op jit(solution)/shard_map/pallas_call | solution.py:723
  67.7 3.0 %shard_map.111 = (f32[9,82,512]{2,1,0:T(8,128)}, f32[32,1024]{1,0:T(8,128)}, f32[1,64]{1,0:T(1,128)}, f32[1,1]{1,0:T(1,128)}, bf16[2,12,128,512]{3,2,1,0:T(8,128)(2,1)}) custom-call(bf16[2,2,48,16,128]{4,3,2,1,0:T(8,128)(2,1)S(1)} %get-tuple-element.14.full, f32[32,1024]{1,0:T(8,128)S(1)} %get-tuple-element.15.noise_in, ...), custom_call_target="tpu_custom_call" | custom-call | tf_op jit(solution)/shard_map/pallas_call | solution.py:744

commit v8 on v7

--- a/solution.py
+++ b/solution.py
@@ -17,7 +17,7 @@
 MESH = pl.DeviceIdType.MESH
 NX, NY, NZ = 4, 4, 8
 TILES = 48
-SEMS = 80
+SEMS = 96
 
 
 class Place:
@@ -102,7 +102,7 @@
     latent, conv_weight, noise_weight, noise_in, var_in, counts_in, target, forward_weight, weight, noise, var_weight, scale, norms, truth, modulation, edges, edge_prod, edge_send, edge_in, rows_beside, normed, inv_std, mixed,
     product, decoded, decoded_half, part_in, cross_in, coef, grads, grads_out, score,
     grad_edge, grad_edge_in, stack, spread, halo, turned, pack, payload, mixed_grad, small,
-    half, from_core, own, first, first_in, own2, second, second_in, over_z,
+    half, from_core, own, first, first_in, own2, second, second_in, z_own, z_out, z_in, over_z,
     small_z, small_x, small_y, small_c, noises, send_sem, recv_sem, local_sem,
 ):
     f32, bf16 = jnp.float32, jnp.bfloat16
@@ -533,12 +533,26 @@
             value = own2[s, me * 3 + t]
             for k in range(3):
                 value = value + second_in[s, k, t].astype(f32)
-            over_z[place.z, s * 3 + t] = value.astype(bf16)
+            z_own[s * 3 + t] = value
+            z_out[s * 3 + t] = value.astype(bf16)
+    for t in (6, 7):
+        z_own[t] = jnp.zeros((16, 128), f32)
+        z_out[t] = jnp.zeros((16, 128), bf16)
+    stage3 = [
+        copies.send(z_out.at[j], z_in.at[k - 1], device) for k, j, device in place.peers("z")
+    ]
+    backward(range(7, 10))
+    for copy in stage3:
+        copy.wait_recv()
+    value = z_own[place.z]
+    for k in range(NZ - 1):
+        value = value + z_in[k].astype(f32)
+    over_z[place.z] = value.astype(bf16)
     stage3 = [
         copies.send(over_z.at[place.z], over_z.at[place.z], device)
         for _, _, device in place.peers("z")
     ]
-    backward(range(7, 12))
+    backward(range(10, 12))
 
     band = jnp.sum(jnp.sum(score[...], axis=1, keepdims=True), axis=0, keepdims=True)
     lanes = lax.broadcasted_iota(jnp.int32, (1, 128), 1)
@@ -562,10 +576,7 @@
     stage4 = []
     for s in range(2):
         for t in range(3):
-            value = over_z[0, s * 3 + t].astype(f32)
-            for z in range(1, NZ):
-                value = value + over_z[z, s * 3 + t].astype(f32)
-            full[core, s, piece(s) + t] = value.astype(bf16)
+            full[core, s, piece(s) + t] = over_z[s * 3 + t]
         stage4.append(gather(s, piece(s), 3, SETS[s][1]))
     for copy in small_copies:
         copy.wait_recv()
@@ -707,7 +718,10 @@
         ((2, 12, 16, 128), f32),
         ((2, 12, 16, 128), bf16),
         ((2, 3, 3, 16, 128), bf16),
-        ((NZ, 6, 16, 128), bf16),
+        ((NZ, 16, 128), f32),
+        ((NZ, 16, 128), bf16),
+        ((NZ - 1, 16, 128), bf16),
+        ((NZ, 16, 128), bf16),
         ((NZ, 24, 128), f32),
         ((4, 24, 128), f32),
         ((4, 24, 128), f32),

time: 70.8 us -> 75.2 us (1.062)
  Pallas kernels: 70 us -> 74.5 us
    pallas_call x1, Pallas kernels: 67 us -> 71.5 us  [per_device(): pl.pallas_call(kernel, out_shape=held, in_specs=[smem] + [anywhere] * 7,...]
where the time goes in v8:
time: 75.2 us
  Pallas kernels  74.5 us (99%)
    pallas_call x1, Pallas kernels, per_device(): pl.pallas_call(kernel, out_shape=held, in_specs=[smem] + [anywhere] * 7,...  71.5 us
    pallas_call x1, Pallas kernels, per_device(): pl.pallas_call(write_kernel, out_shape=(jax.ShapeDtypeStruct((9, V, C), f...  2.98 us

profile of v8, /device:TPU:1, one launch (start us, length us, event | category | flops | bytes accessed | tf_op | source)
XLA Modules:
  0.0 75.2 jit_solution(10735556372543052508)
XLA Ops:
  0.6 71.5 %shard_map.110 = (bf16[2,2,48,16,128]{4,3,2,1,0:T(8,128)(2,1)S(1)}, f32[32,1024]{1,0:T(8,128)S(1)}, f32[8,128]{1,0:T(8,128)S(1)}, bf16[2,12,128,512]{3,2,1,0:T(8,128)(2,1)S(1)}) custom-call(s32[64]{0:T(128)} %counts.1, bf16[2,12,128,512]{3,2,1,0:T(8,128)(2,1)} %latent_hbm.1, bf16[9,82,512]{2,1,0:T(8,128)(2,1)} %conv_hbm.1, f32[32,1024]{1,0:T(8,128)} %noise_weight_hbm.1, ...), custom_call_target="tpu_custom_call" | custom-call | tf_op jit(solution)/shard_map/pallas_call | solution.py:737
  72.2 3.0 %shard_map.111 = (f32[9,82,512]{2,1,0:T(8,128)}, f32[32,1024]{1,0:T(8,128)}, f32[1,64]{1,0:T(1,128)}, f32[1,1]{1,0:T(1,128)}, bf16[2,12,128,512]{3,2,1,0:T(8,128)(2,1)}) custom-call(bf16[2,2,48,16,128]{4,3,2,1,0:T(8,128)(2,1)S(1)} %get-tuple-element.14.full, f32[32,1024]{1,0:T(8,128)S(1)} %get-tuple-element.15.noise_in, ...), custom_call_target="tpu_custom_call" | custom-call | tf_op jit(solution)/shard_map/pallas_call | solution.py:758

commit v9 on v7

--- a/solution.py
+++ b/solution.py
@@ -71,7 +71,7 @@
 
 
 def greet(place):
-    devices = [d for axis in ("x", "y", "z", "core") for _, _, d in place.peers(axis)]
+    devices = [d for axis in ("z", "x", "y", "core") for _, _, d in place.peers(axis)]
     devices.append(place.at(y=place.y + 1 - 2 * lax.rem(place.y, 2), core=1 - place.core))
     devices += [place.band(1), place.band(-1)]
     barrier = pltpu.get_barrier_semaphore()
@@ -190,16 +190,7 @@
             value = fold(edge_prod, slice(i * LON, (i + 1) * LON))
             edge_send[side, i * VP : (i + 1) * VP, :] = value
         edge_copies.append(copies.send(edge_send.at[side], edge_in.at[side], place.band(step)))
-    row_copies = [
-        copies.send(edges.at[side], rows_beside.at[side], place.band(step))
-        for side, step in ((0, -1), (1, 1))
-    ]
-
-    noises[place.member] = noise[...]
-    noise_copies = [
-        copies.send(noises.at[place.member], noises.at[place.member], device)
-        for device in (partner, place.at(y=beside), place.at(y=beside, core=1 - core))
-    ]
+
     for load in loads[4:]:
         load.wait()
 
@@ -280,6 +271,16 @@
                 )
                 part_copies.append(copies.send(decoded.at[pair], part_in.at[n], partner))
 
+    row_copies = [
+        copies.send(edges.at[side], rows_beside.at[side], place.band(step))
+        for side, step in ((0, -1), (1, 1))
+    ]
+    noises[place.member] = noise[...]
+    noise_copies = [
+        copies.send(noises.at[place.member], noises.at[place.member], device)
+        for device in (partner, place.at(y=beside), place.at(y=beside, core=1 - core))
+    ]
+
     def spread_row(value, slot):
         stack[slot, 0:VP, :] = rolled(value, -1)
         stack[slot, V : V + VP, :] = value
@@ -320,6 +321,9 @@
             value = nn_dot(jnp.concatenate([spread[pair, 0], spread[pair, 1]], axis=1), rows_in)
             if not begin:
                 value = value + payload[a * KP : (a + 1) * KP, :]
+            if last and a == 2:
+                for copy in row_copies:
+                    copy.wait_recv()
             if last and a != 1:
                 value = value + weigh_edge(a)
             payload[a * KP : (a + 1) * KP, :] = value
@@ -420,8 +424,6 @@
         grad_edge[side] = stack[side, :PAIR].astype(bf16)
         grad_edge_copies.append(copies.send(grad_edge.at[side], grad_edge_in.at[side], place.band(step)))
 
-    for copy in row_copies:
-        copy.wait_recv()
     weigh((1 - core) * 3 + 2, last=True)
 
     small[...] = jnp.zeros_like(small)

time: 70.8 us -> 73.5 us (1.038)
  Pallas kernels: 70 us -> 72.8 us
    pallas_call x1, Pallas kernels: 67 us -> 69.8 us  [per_device(): pl.pallas_call(kernel, out_shape=held, in_specs=[smem] + [anywhere] * 7,...]
where the time goes in v9:
time: 73.5 us; the launch traced here: 73.4 us
  Pallas kernels  72.8 us (99%)
    pallas_call x1, Pallas kernels, per_device(): pl.pallas_call(kernel, out_shape=held, in_specs=[smem] + [anywhere] * 7,...  69.8 us
    pallas_call x1, Pallas kernels, per_device(): pl.pallas_call(write_kernel, out_shape=(jax.ShapeDtypeStruct((9, V, C), f...  2.98 us

profile of v9, /device:TPU:1, one launch (start us, length us, event | category | flops | bytes accessed | tf_op | source)
XLA Modules:
  0.0 73.4 jit_solution(14216377943084333115)
XLA Ops:
  0.6 69.8 %shard_map.110 = (bf16[2,2,48,16,128]{4,3,2,1,0:T(8,128)(2,1)S(1)}, f32[32,1024]{1,0:T(8,128)S(1)}, f32[8,128]{1,0:T(8,128)S(1)}, bf16[2,12,128,512]{3,2,1,0:T(8,128)(2,1)S(1)}) custom-call(s32[64]{0:T(128)} %counts.1, bf16[2,12,128,512]{3,2,1,0:T(8,128)(2,1)} %latent_hbm.1, bf16[9,82,512]{2,1,0:T(8,128)(2,1)} %conv_hbm.1, f32[32,1024]{1,0:T(8,128)} %noise_weight_hbm.1, ...), custom_call_target="tpu_custom_call" | custom-call | tf_op jit(solution)/shard_map/pallas_call | solution.py:725
  70.5 3.0 %shard_map.111 = (f32[9,82,512]{2,1,0:T(8,128)}, f32[32,1024]{1,0:T(8,128)}, f32[1,64]{1,0:T(1,128)}, f32[1,1]{1,0:T(1,128)}, bf16[2,12,128,512]{3,2,1,0:T(8,128)(2,1)}) custom-call(bf16[2,2,48,16,128]{4,3,2,1,0:T(8,128)(2,1)S(1)} %get-tuple-element.14.full, f32[32,1024]{1,0:T(8,128)S(1)} %get-tuple-element.15.noise_in, ...), custom_call_target="tpu_custom_call" | custom-call | tf_op jit(solution)/shard_map/pallas_call | solution.py:746

commit v10 on v7

--- a/solution.py
+++ b/solution.py
@@ -190,11 +190,7 @@
             value = fold(edge_prod, slice(i * LON, (i + 1) * LON))
             edge_send[side, i * VP : (i + 1) * VP, :] = value
         edge_copies.append(copies.send(edge_send.at[side], edge_in.at[side], place.band(step)))
-    row_copies = [
-        copies.send(edges.at[side], rows_beside.at[side], place.band(step))
-        for side, step in ((0, -1), (1, 1))
-    ]
-
+    row_copy = copies.send(edges.at[0], rows_beside, place.band(-1))
     noises[place.member] = noise[...]
     noise_copies = [
         copies.send(noises.at[place.member], noises.at[place.member], device)
@@ -298,14 +294,26 @@
         left = []
         for i in range(2):
             if a == 0:
-                value = jnp.where(has_prev, spread[0, i, :, :LON], jnp.zeros((KP, LON), bf16))
+                value = halo[0, i]
             else:
                 both = spread[lax.div(final, 2), i]
                 value = jnp.where(lax.rem(final, 2) == 1, both[:, LON:], both[:, :LON])
                 value = jnp.where(has_next, value, jnp.zeros((KP, LON), bf16))
             left.append(value)
-        side = 1 if a == 0 else 0
-        return nn_dot(jnp.concatenate(left, axis=1), rows_beside[side].reshape(2 * LON, C))
+        right = edges[1] if a == 0 else rows_beside[...]
+        return nn_dot(jnp.concatenate(left, axis=1), right.reshape(2 * LON, C))
+
+    def spread_halo(side, there):
+        grad_edge_copies[side].wait_recv()
+        both = jnp.where(there, grad_edge_in[side].astype(f32), 0.0)
+        for i in range(2):
+            halo[side, i] = spread_row(both[i * VP : (i + 1) * VP], 2 * side + i)
+
+    def send_edge(side, rows, step):
+        for i in range(2):
+            stack[side, i * VP : (i + 1) * VP, :] = rows[i]
+        grad_edge[side] = stack[side, :PAIR].astype(bf16)
+        grad_edge_copies.append(copies.send(grad_edge.at[side], grad_edge_in.at[side], place.band(step)))
 
     def weigh(pair, begin=False, last=False):
         for i in range(2):
@@ -340,7 +348,7 @@
                 turned[i, slot] = jnp.where(count + 1 == slot, trailing, turned[i, slot])
 
     score[...] = jnp.zeros_like(score)
-    grad_copies = []
+    grad_copies, grad_edge_copies = [], []
     for n in range(3):
         pair = core * 3 + n
         for r in range(2):
@@ -348,6 +356,8 @@
             truth[r * VP : r * VP + V, :] = target[2 * pair + r].astype(f32)
         if n > 0:
             grad_copies[n - 1].wait_recv()
+            if n == 1:
+                send_edge(0, [grads[0, i].astype(f32)[:VP] for i in range(2)], -1)
             weigh((1 - core) * 3 + n - 1)
         if n == 2:
             for a in range(3):
@@ -409,19 +419,13 @@
         weigh(pair, begin=n == 0)
     grad_copies[2].wait_recv()
 
+    tails = []
     for i in range(2):
-        edge_pair = grads[lax.div(final, 2), i].astype(f32)
-        head = grads[0, i].astype(f32)[:VP]
-        tail = jnp.where(lax.rem(final, 2) == 1, edge_pair[VP:], edge_pair[:VP])
-        stack[0, i * VP : (i + 1) * VP, :] = head
-        stack[1, i * VP : (i + 1) * VP, :] = tail
-    grad_edge_copies = []
-    for side, step in ((0, -1), (1, 1)):
-        grad_edge[side] = stack[side, :PAIR].astype(bf16)
-        grad_edge_copies.append(copies.send(grad_edge.at[side], grad_edge_in.at[side], place.band(step)))
-
-    for copy in row_copies:
-        copy.wait_recv()
+        both = grads[lax.div(final, 2), i].astype(f32)
+        tails.append(jnp.where(lax.rem(final, 2) == 1, both[VP:], both[:VP]))
+    send_edge(1, tails, 1)
+    row_copy.wait_recv()
+    spread_halo(0, has_next)
     weigh((1 - core) * 3 + 2, last=True)
 
     small[...] = jnp.zeros_like(small)
@@ -500,12 +504,7 @@
     stage1 = [scatter(0, first, first_in, 12, SETS[0][0])]
     take_from_core(2)
     stage1.append(scatter(1, first, first_in, 12, SETS[1][0]))
-    for copy in grad_edge_copies:
-        copy.wait_recv()
-    for side, there in ((1, has_prev), (0, has_next)):
-        both = jnp.where(there, grad_edge_in[side].astype(f32), 0.0)
-        for i in range(2):
-            halo[side, i] = spread_row(both[i * VP : (i + 1) * VP], 2 * side + i)
+    spread_halo(1, has_prev)
     turn(core * 3 + 2)
     turn((1 - core) * 3 + 2)
     turn_halo()
@@ -676,7 +675,7 @@
         ((3 * VA, 2 * LON), f32),
         ((2, PAIR, LON), f32),
         ((2, PAIR, LON), f32),
-        ((2, 2, LON, C), bf16),
+        ((2, LON, C), bf16),
         ((2, BAND, LON, C), f32),
         ((2, BAND, LON, LON), f32),
         ((2, BAND + 2, LON, C), bf16),

time: 70.8 us -> 69.9 us (0.987)
  Pallas kernels: 70 us -> 69 us
    pallas_call x1, Pallas kernels: 67 us -> 66 us  [per_device(): pl.pallas_call(kernel, out_shape=held, in_specs=[smem] + [anywhere] * 7,...]
where the time goes in v10:
time: 69.9 us; the launch traced here: 69.6 us
  Pallas kernels  69 us (99%)
    pallas_call x1, Pallas kernels, per_device(): pl.pallas_call(kernel, out_shape=held, in_specs=[smem] + [anywhere] * 7,...  66 us
    pallas_call x1, Pallas kernels, per_device(): pl.pallas_call(write_kernel, out_shape=(jax.ShapeDtypeStruct((9, V, C), f...  2.98 us

profile of v10, /device:TPU:1, one launch (start us, length us, event | category | flops | bytes accessed | tf_op | source)
XLA Modules:
  0.0 69.6 jit_solution(6509893511306600920)
XLA Ops:
  0.6 66.0 %shard_map.110 = (bf16[2,2,48,16,128]{4,3,2,1,0:T(8,128)(2,1)S(1)}, f32[32,1024]{1,0:T(8,128)S(1)}, f32[8,128]{1,0:T(8,128)S(1)}, bf16[2,12,128,512]{3,2,1,0:T(8,128)(2,1)S(1)}) custom-call(s32[64]{0:T(128)} %counts.1, bf16[2,12,128,512]{3,2,1,0:T(8,128)(2,1)} %latent_hbm.1, bf16[9,82,512]{2,1,0:T(8,128)(2,1)} %conv_hbm.1, f32[32,1024]{1,0:T(8,128)} %noise_weight_hbm.1, ...), custom_call_target="tpu_custom_call" | custom-call | tf_op jit(solution)/shard_map/pallas_call | solution.py:722
  66.6 3.0 %shard_map.111 = (f32[9,82,512]{2,1,0:T(8,128)}, f32[32,1024]{1,0:T(8,128)}, f32[1,64]{1,0:T(1,128)}, f32[1,1]{1,0:T(1,128)}, bf16[2,12,128,512]{3,2,1,0:T(8,128)(2,1)}) custom-call(bf16[2,2,48,16,128]{4,3,2,1,0:T(8,128)(2,1)S(1)} %get-tuple-element.14.full, f32[32,1024]{1,0:T(8,128)S(1)} %get-tuple-element.15.noise_in, ...), custom_call_target="tpu_custom_call" | custom-call | tf_op jit(solution)/shard_map/pallas_call | solution.py:743
